TPU v7x, 32 devices: a whole 2x2x4 slice. The times are simulated.
32 devices in a mesh: seq: 8 (over y, x, core), chan: 4 (over z).
Axes of the slice: x: 2, y: 2, z: 4, core: 2. Of those that a mesh axis runs over, the one named last changes fastest.
Arguments:
- queries: bfloat16 [64, 32768], P('chan', 'seq'), may hold values from -6 to 6
- key_proj: bfloat16 [64, 32768], P('chan', 'seq'), may hold values from -6 to 6
- value_proj: bfloat16 [64, 32768], P('chan', 'seq'), may hold values from -6 to 6
- cotangent: bfloat16 [64, 32768], P('chan', 'seq'), may hold values from -6 to 6
- filter_taps: bfloat16 [64, 32768], P('chan', 'seq'), may hold values from -0.032958984 to 0.032958984
- skip_gain: float32 [64], P('chan'), may hold values from -6 to 6
Outputs:
- grad_query: bfloat16 [64, 32768], P('chan', 'seq')
- grad_key: bfloat16 [64, 32768], P('chan', 'seq')
- grad_value: bfloat16 [64, 32768], P('chan', 'seq')
- grad_filter: bfloat16 [64, 32768], P('chan', 'seq')
- grad_skip: float32 [64], P('chan')
All inputs are finite; a program needn't handle non-finite values.
Results may differ from a plain program's by a relative error of at most 0.001.
Values may be sent and summed in bfloat16 or wider, within the bound.
A program may use at most 64 MiB of HBM per device.

v0:
```python
import math

import jax
import jax.numpy as jnp
from jax import lax
from jax.sharding import PartitionSpec as P

highest = lax.Precision.HIGHEST


def from_partner(block, axis, stride):
    count = lax.axis_size(axis)
    route = []
    for low in range(count):
        high = low | 1 << stride
        if high != low and high < count:
            route += [(low, high), (high, low)]
    return lax.ppermute(block, axis, route)


def complex_product(pattern, left_re, left_im, right_re, right_im):
    real_real = jnp.einsum(pattern, left_re, right_re, precision=highest)
    imag_imag = jnp.einsum(pattern, left_im, right_im, precision=highest)
    real_imag = jnp.einsum(pattern, left_re, right_im, precision=highest)
    imag_real = jnp.einsum(pattern, left_im, right_re, precision=highest)
    return (real_real - imag_imag, real_imag + imag_real)


def rotate(real_in, imag_in, angle_val):
    cosine = jnp.cos(angle_val)
    sine_val = jnp.sin(angle_val)
    return (real_in * cosine - imag_in * sine_val, real_in * sine_val + imag_in * cosine)


def dft_table(length, direction):
    counter = jnp.arange(length, dtype=jnp.int32)
    phase_idx = counter[:, None] * counter[None, :] % length
    angle_val = direction * 2.0 * math.pi / length * phase_idx.astype(jnp.float32)
    return (jnp.cos(angle_val), jnp.sin(angle_val))


def twiddle_angle(row_count, radix_len, length, direction):
    phase_idx = (
        jnp.arange(row_count, dtype=jnp.int32)[:, None]
        * jnp.arange(radix_len, dtype=jnp.int32)[None, :]
        % length
    )
    return direction * 2.0 * math.pi / length * phase_idx.astype(jnp.float32)


def local_forward(real_in, imag_in):
    length = real_in.shape[-1]
    radix_len = math.gcd(length, 512)
    row_count = length // radix_len
    new_shape = real_in.shape[:-1] + (row_count, radix_len)
    first_re, first_im = dft_table(row_count, -1.0)
    work_re, work_im = complex_product(
        "ab,...bj->...aj",
        first_re,
        first_im,
        real_in.reshape(new_shape),
        imag_in.reshape(new_shape),
    )
    work_re, work_im = rotate(work_re, work_im, twiddle_angle(row_count, radix_len, length, -1.0))
    second_re, second_im = dft_table(radix_len, -1.0)
    work_re, work_im = complex_product("...aj,jk->...ak", work_re, work_im, second_re, second_im)
    return (work_re.reshape(real_in.shape), work_im.reshape(real_in.shape))


def local_inverse(real_in, imag_in):
    length = real_in.shape[-1]
    radix_len = math.gcd(length, 512)
    row_count = length // radix_len
    new_shape = real_in.shape[:-1] + (row_count, radix_len)
    second_re, second_im = dft_table(radix_len, 1.0)
    work_re, work_im = complex_product(
        "...ak,kj->...aj",
        real_in.reshape(new_shape),
        imag_in.reshape(new_shape),
        second_re,
        second_im,
    )
    work_re, work_im = rotate(work_re, work_im, twiddle_angle(row_count, radix_len, length, 1.0))
    first_re, first_im = dft_table(row_count, 1.0)
    work_re, work_im = complex_product("ab,...aj->...bj", first_re, first_im, work_re, work_im)
    return (work_re.reshape(real_in.shape), work_im.reshape(real_in.shape))


def bit_reverse(seq_index, bit_total):
    reversed_idx = jnp.zeros_like(seq_index)
    for bit_level in range(bit_total):
        reversed_idx = reversed_idx | (seq_index >> bit_level & 1) << bit_total - 1 - bit_level
    return reversed_idx


def frequency_angle(frequencies, lane_count, padded_len, direction):
    lanes = jnp.arange(lane_count, dtype=jnp.int32)
    parity = jnp.arange(2, dtype=jnp.int32)
    spectral = 2 * frequencies[None, :] + parity[:, None]
    phase_idx = spectral[:, :, None] * lanes[None, None, :] % padded_len
    angle_val = direction * 2.0 * math.pi / padded_len * phase_idx.astype(jnp.float32)
    return angle_val[:, None, None]


def to_spectrum(signals, blocks, seq_index, seq_count, block_total):
    lane_count = signals.shape[-1]
    padded_len = 2 * block_total * lane_count
    half_turn = (math.pi / block_total * blocks.astype(jnp.float32))[:, None]
    real_part = jnp.stack([signals, signals * jnp.cos(half_turn)])
    imag_part = jnp.stack([jnp.zeros_like(signals), -signals * jnp.sin(half_turn)])
    bit_total = seq_count.bit_length() - 1
    for bit_level in reversed(range(bit_total)):
        half_span = 1 << bit_level
        other_re, other_im = from_partner((real_part, imag_part), "seq", bit_level)
        position = seq_index % (2 * half_span)
        is_upper = position < half_span
        sum_re = jnp.where(is_upper, real_part + other_re, other_re - real_part)
        sum_im = jnp.where(is_upper, imag_part + other_im, other_im - imag_part)
        angle_val = jnp.where(
            is_upper, 0.0, -math.pi * (position % half_span).astype(jnp.float32) / half_span
        )
        real_part, imag_part = rotate(sum_re, sum_im, angle_val)
    frequencies = bit_reverse(seq_index, bit_total)[None]
    real_part, imag_part = rotate(
        real_part, imag_part, frequency_angle(frequencies, lane_count, padded_len, -1.0)
    )
    return (local_forward(real_part, imag_part), frequencies)


def to_signal(real_part, imag_part, frequencies, blocks, seq_index, seq_count, block_total):
    lane_count = real_part.shape[-1]
    padded_len = 2 * block_total * lane_count
    real_part, imag_part = local_inverse(real_part, imag_part)
    real_part, imag_part = rotate(
        real_part, imag_part, frequency_angle(frequencies, lane_count, padded_len, 1.0)
    )
    bit_total = seq_count.bit_length() - 1
    for bit_level in range(bit_total):
        half_span = 1 << bit_level
        other_re, other_im = from_partner((real_part, imag_part), "seq", bit_level)
        position = seq_index % (2 * half_span)
        is_upper = position < half_span
        taken_re = jnp.where(is_upper, other_re, real_part)
        taken_im = jnp.where(is_upper, other_im, imag_part)
        base_re = jnp.where(is_upper, real_part, other_re)
        base_im = jnp.where(is_upper, imag_part, other_im)
        angle_val = math.pi * (position % half_span).astype(jnp.float32) / half_span
        turned_re, turned_im = rotate(taken_re, taken_im, angle_val)
        flip_sign = jnp.where(is_upper, 1.0, -1.0)
        real_part = base_re + flip_sign * turned_re
        imag_part = base_im + flip_sign * turned_im
    half_turn = (math.pi / block_total * blocks.astype(jnp.float32))[:, None]
    combined = real_part[0] + real_part[1] * jnp.cos(half_turn) - imag_part[1] * jnp.sin(half_turn)
    return combined / padded_len


def local(queries, key_proj, value_proj, cotangent, filter_taps, skip_gain):
    seq_count = lax.axis_size("seq")
    seq_index = lax.axis_index("seq")
    tok_local = queries.shape[1]
    tokens_all = seq_count * tok_local
    norm_scale = 1.0 / math.sqrt(tokens_all)
    chan_input = queries.shape[0]
    query_in, key_in, value_in, cot_in, taps_in = (
        queries,
        key_proj,
        value_proj,
        cotangent,
        filter_taps,
    )
    blocks = seq_index[None]
    block_shape = (chan_input, blocks.shape[0], tok_local)
    query_f = query_in.reshape(block_shape).astype(jnp.float32)
    key_f = key_in.reshape(block_shape).astype(jnp.float32)
    value_f = value_in.reshape(block_shape).astype(jnp.float32)
    cot_f = cot_in.reshape(block_shape).astype(jnp.float32)
    kernel = taps_in.reshape(block_shape).astype(jnp.float32)
    mixed = key_f * value_f
    gated = cot_f * query_f
    signals = jnp.stack([mixed, gated, kernel])
    (spec_re, spec_im), frequencies = to_spectrum(signals, blocks, seq_index, seq_count, seq_count)
    mix_re, mix_im = (spec_re[:, 0], spec_im[:, 0])
    grad_re, grad_im = (spec_re[:, 1], spec_im[:, 1])
    ker_re, ker_im = (spec_re[:, 2], spec_im[:, 2])
    prod_re = jnp.stack(
        [
            ker_re * mix_re - ker_im * mix_im,
            ker_re * grad_re + ker_im * grad_im,
            grad_re * mix_re + grad_im * mix_im,
        ],
        1,
    )
    prod_im = jnp.stack(
        [
            ker_re * mix_im + ker_im * mix_re,
            ker_re * grad_im - ker_im * grad_re,
            grad_im * mix_re - grad_re * mix_im,
        ],
        1,
    )
    results = to_signal(prod_re, prod_im, frequencies, blocks, seq_index, seq_count, seq_count)
    convolved, carried, lag_grad = (results[0], results[1], results[2])
    skip_col = skip_gain[:, None, None]
    grad_query = (cot_f * (convolved + skip_col * mixed)).astype(jnp.bfloat16)
    grad_mixed = carried + skip_col * gated
    grad_key = (grad_mixed * value_f).astype(jnp.bfloat16)
    grad_value = (grad_mixed * key_f).astype(jnp.bfloat16)
    grad_filter = (lag_grad * norm_scale).astype(jnp.bfloat16)
    skip_part = jnp.sum(gated * mixed, axis=(1, 2))
    flat_shape = (chan_input, tok_local)
    grad_query = grad_query.reshape(flat_shape)
    grad_key = grad_key.reshape(flat_shape)
    grad_value = grad_value.reshape(flat_shape)
    grad_filter = grad_filter.reshape(flat_shape)
    skip_sum = lax.psum(skip_part, "seq")
    return (grad_query, grad_key, grad_value, grad_filter, skip_sum * norm_scale)


def solution(mesh):
    return jax.shard_map(
        local,
        mesh=mesh,
        in_specs=(
            P("chan", "seq"),
            P("chan", "seq"),
            P("chan", "seq"),
            P("chan", "seq"),
            P("chan", "seq"),
            P("chan"),
        ),
        out_specs=(
            P("chan", "seq"),
            P("chan", "seq"),
            P("chan", "seq"),
            P("chan", "seq"),
            P("chan"),
        ),
        check_vma=False,
    )
```

profile of v0, /device:TPU:0, one launch (start us, length us, event | category | flops | bytes accessed | tf_op | source)
XLA Modules:
  0.0 423.4 jit_solution(3640477749038421557)
XLA Ops:
  1.7 1.2 fusion.69
  3.1 1.3 pad_maximum_fusion
  4.4 3.0 collective-permute-start
  7.4 1.3 stack.65
  8.8 34.1 %collective-permute-done = f32[2,3,16,1,4096]{4,2,3,1,0:T(8,128)} collective-permute-done((f32[2,3,16,1,4096]{4,2,3,1,0:T(8,128)}, f32[2,3,16,1,4096]{4,2,3,1,0:T(8,128)}, u32[]{:S(2)}, u32[]{:S(2)}) %collective-permute-start) | collective-permute-done | bytes 1572896 | tf_op jit(solution)/shard_map/ppermute | solution.py:18
  42.9 32.9 %collective-permute-done.1 = f32[2,3,16,1,4096]{4,2,3,1,0:T(8,128)} collective-permute-done((f32[2,3,16,1,4096]{4,2,3,1,0:T(8,128)}, f32[2,3,16,1,4096]{4,2,3,1,0:T(8,128)}, u32[]{:S(2)}, u32[]{:S(2)}) %collective-permute-start.1) | collective-permute-done | bytes 1572896 | tf_op jit(solution)/shard_map/ppermute | solution.py:18
  75.8 4.2 multiply_add_fusion.9
  80.0 1.7 collective-permute-start.2
  82.1 35.4 %collective-permute-done.2 = f32[2,3,16,1,4096]{4,2,3,1,0:T(8,128)S(1)} collective-permute-done((f32[2,3,16,1,4096]{4,2,3,1,0:T(8,128)}, f32[2,3,16,1,4096]{4,2,3,1,0:T(8,128)S(1)}, u32[]{:S(2)}, u32[]{:S(2)}) %collective-permute-start.2) | collective-permute-done | bytes 1572896 | tf_op jit(solution)/shard_map/ppermute | solution.py:18
  117.5 1.2 copy-done.3
  118.7 30.9 %collective-permute-done.3 = f32[2,3,16,1,4096]{4,2,3,1,0:T(8,128)} collective-permute-done((f32[2,3,16,1,4096]{4,2,3,1,0:T(8,128)}, f32[2,3,16,1,4096]{4,2,3,1,0:T(8,128)}, u32[]{:S(2)}, u32[]{:S(2)}) %collective-permute-start.3) | collective-permute-done | bytes 1572896 | tf_op jit(solution)/shard_map/ppermute | solution.py:18
  149.6 3.5 multiply_subtract_fusion.3
  154.0 1.7 multiply_cosine_fusion.6
  156.7 2.2 collective-permute-done.5
  158.9 2.7 multiply_subtract_fusion.1
  161.9 1.1 copy.34
  164.1 1.6 fusion.90
  165.6 1.6 fusion.88
  167.2 1.7 convolution_subtract_fusion
  168.9 1.7 convolution_add_fusion
  170.6 6.8 %fusion.24 = f32[2,3,16,8,512]{4,3,2,1,0:T(8,128)S(1)} fusion(f32[2,3,16,512,8]{3,4,2,1,0:T(8,128)S(1)} %convolution_add_fusion, f32[2,3,16,512,8]{3,4,2,1,0:T(8,128)S(1)} %convolution_subtract_fusion, f32[8,512]{1,0:T(8,128)S(1)} %get-tuple-element.45, f32[8,512]{1,0:T(8,128)S(1)} %get-tuple-element.46), kind=kOutput, calls=%fused_computation.61 | convolution fusion | flops 2420768768 | bytes 4751360 | tf_op jit(solution)/shard_map/...aj,jk->...ak/dot_general | solution.py:22
  177.4 7.9 %fusion.26 = f32[2,3,16,8,512]{4,3,2,1,0:T(8,128)} fusion(f32[2,3,16,512,8]{3,4,2,1,0:T(8,128)S(1)} %convolution_add_fusion, f32[2,3,16,512,8]{3,4,2,1,0:T(8,128)S(1)} %convolution_subtract_fusion, f32[8,512]{1,0:T(8,128)S(1)} %get-tuple-element.45, f32[8,512]{1,0:T(8,128)S(1)} %get-tuple-element.46), kind=kOutput, calls=%fused_computation.63 | convolution fusion | flops 2420768768 | bytes 4751360 | tf_op jit(solution)/shard_map/...aj,jk->...ak/dot_general | solution.py:24
  185.4 6.7 %fusion.9 = f32[2,3,16,8,512]{4,3,2,1,0:T(8,128)S(1)} fusion(f32[2,3,16,8,512]{4,3,2,1,0:T(8,128)S(1)} %fusion.24, f32[2,3,16,512,8]{3,4,2,1,0:T(8,128)S(1)} %convolution_add_fusion, f32[2,3,16,512,8]{3,4,2,1,0:T(8,128)S(1)} %convolution_subtract_fusion, f32[8,512]{1,0:T(8,128)S(1)} %get-tuple-element.45, f32[8,512]{1,0:T(8,128)S(1)} %get-tuple-element.46), kind=kOutput, calls=%fused_computation.48 | convolution fusion | flops 2421161984 | bytes 6324224 | tf_op jit(solution)/shard_map/...aj,jk->...ak/dot_general | solution.py:23
  192.4 9.8 %fusion.12 = f32[2,3,16,8,512]{4,3,2,1,0:T(8,128)} fusion(f32[2,3,16,8,512]{4,3,2,1,0:T(8,128)} %fusion.26, f32[2,3,16,512,8]{3,4,2,1,0:T(8,128)} %copy-done.5, f32[2,3,16,512,8]{3,4,2,1,0:T(8,128)} %copy-done.4, f32[8,512]{1,0:T(8,128)S(1)} %get-tuple-element.45, f32[8,512]{1,0:T(8,128)S(1)} %get-tuple-element.46), kind=kOutput, calls=%fused_computation.49 | convolution fusion | flops 2421161984 | bytes 6324224 | tf_op jit(solution)/shard_map/...aj,jk->...ak/dot_general | solution.py:25
  202.2 2.0 reshape.647
  205.6 6.5 %fusion.16 = f32[2,3,16,8,512]{4,3,2,1,0:T(8,128)S(1)} fusion(f32[2,1,16,1,8,512]{5,4,2,1,0,3:T(8,128)S(1)} %bitcast.257, f32[2,1,16,1,8,512]{5,4,2,1,0,3:T(8,128)S(1)} %bitcast.255, f32[2,1,16,1,8,512]{5,4,2,1,0,3:T(8,128)S(1)} %bitcast.251), kind=kOutput, calls=%fused_computation.53 | convolution fusion | flops 2420375552 | bytes 3145728 | tf_op jit(solution)/shard_map/...ak,kj->...aj/dot_general | solution.py:22
  212.1 6.7 %fusion.15 = f32[2,3,16,8,512]{4,3,2,1,0:T(8,128)S(1)} fusion(f32[2,1,16,1,8,512]{5,4,2,1,0,3:T(8,128)S(1)} %bitcast.258, f32[2,1,16,1,8,512]{5,4,2,1,0,3:T(8,128)S(1)} %bitcast.256, f32[2,1,16,1,8,512]{5,4,2,1,0,3:T(8,128)S(1)} %bitcast.252), kind=kOutput, calls=%fused_computation.52 | convolution fusion | flops 2420375552 | bytes 3145728 | tf_op jit(solution)/shard_map/...ak,kj->...aj/dot_general | solution.py:24
  219.7 6.5 %convolution_subtract_fusion.1 = f32[2,3,16,8,512]{4,3,2,1,0:T(8,128)S(1)} fusion(f32[2,3,16,8,512]{4,3,2,1,0:T(8,128)S(1)} %fusion.16, f32[2,1,16,1,8,512]{5,4,2,1,0,3:T(8,128)S(1)} %bitcast.249, f32[2,1,16,1,8,512]{5,4,2,1,0,3:T(8,128)S(1)} %bitcast.247, f32[2,1,16,1,8,512]{5,4,2,1,0,3:T(8,128)S(1)} %bitcast.253), kind=kOutput, calls=%fused_computation.51 | convolution fusion | flops 2420768768 | bytes 4718592 | tf_op jit(solution)/shard_map/...ak,kj->...aj/dot_general | solution.py:23
  226.3 6.7 %convolution_add_fusion.1 = f32[2,3,16,8,512]{4,3,2,1,0:T(8,128)S(1)} fusion(f32[2,3,16,8,512]{4,3,2,1,0:T(8,128)S(1)} %fusion.15, f32[2,1,16,1,8,512]{5,4,2,1,0,3:T(8,128)S(1)} %bitcast.250, f32[2,1,16,1,8,512]{5,4,2,1,0,3:T(8,128)S(1)} %bitcast.248, f32[2,1,16,1,8,512]{5,4,2,1,0,3:T(8,128)S(1)} %bitcast.254), kind=kOutput, calls=%fused_computation.50 | convolution fusion | flops 2420768768 | bytes 4718592 | tf_op jit(solution)/shard_map/...ak,kj->...aj/dot_general | solution.py:25
  233.0 1.6 fusion.56
  234.7 2.9 fusion.57
  237.5 3.0 subtract_bitcast_fusion
  240.5 2.8 reshape.650
  243.3 4.4 %add_bitcast_fusion = f32[2,3,16,1,8,512]{5,4,2,1,0,3:T(8,128)} fusion(f32[2,3,16,512,8]{3,4,2,1,0:T(8,128)} %fusion.57, f32[2,3,16,8,512]{4,3,2,1,0:T(8,128)S(1)} %convolution_add_fusion.1, f32[2,3,16,8,512]{4,3,2,1,0:T(8,128)S(1)} %convolution_subtract_fusion.1, f32[8,512]{1,0:T(8,128)S(1)} %get-tuple-element.47, f32[8,512]{1,0:T(8,128)S(1)} %get-tuple-element.48), kind=kOutput, calls=%fused_computation.25 | convolution fusion | flops 39322496 | bytes 6324224 | tf_op jit(solution)/shard_map/ab,...aj->...bj/dot_general | solution.py:25
  247.7 2.6 reshape.651
  250.3 2.3 fusion
  253.2 3.0 collective-permute-done.6
  256.2 2.2 collective-permute-done.7
  258.5 3.5 multiply_add_fusion.4
  261.9 1.5 collective-permute-start.8
  264.2 35.2 %collective-permute-done.8 = f32[2,3,16,1,4096]{4,2,3,1,0:T(8,128)} collective-permute-done((f32[2,3,16,1,4096]{4,2,3,1,0:T(8,128)S(1)}, f32[2,3,16,1,4096]{4,2,3,1,0:T(8,128)}, u32[]{:S(2)}, u32[]{:S(2)}) %collective-permute-start.8) | collective-permute-done | bytes 1572896 | tf_op jit(solution)/shard_map/ppermute | solution.py:18
  299.3 32.9 %collective-permute-done.9 = f32[2,3,16,1,4096]{4,2,3,1,0:T(8,128)} collective-permute-done((f32[2,3,16,1,4096]{4,2,3,1,0:T(8,128)S(1)}, f32[2,3,16,1,4096]{4,2,3,1,0:T(8,128)}, u32[]{:S(2)}, u32[]{:S(2)}) %collective-permute-start.9) | collective-permute-done | bytes 1572896 | tf_op jit(solution)/shard_map/ppermute | solution.py:18
  332.3 4.3 %multiply_add_fusion.2 = (f32[2,3,16,1,4096]{4,2,3,1,0:T(8,128)}, f32[2,3,16,1,4096]{4,2,3,1,0:T(8,128)S(1)}) fusion(f32[2,3,16,1,4096]{4,2,3,1,0:T(8,128)S(1)} %get-tuple-element.12, f32[2,3,16,1,4096]{4,2,3,1,0:T(8,128)} %collective-permute-done.8, f32[]{:T(128)S(6)} %sin.88, f32[]{:T(128)S(6)} %cos.88, f32[]{:T(128)S(6)} %select_n.270, pred[]{:T(512)S(6)} %lt.125, ...), kind=kLoop, calls=%fused_computation.22 | loop fusion | flops 5505024 | bytes 9437197 | tf_op jit(solution)/shard_map/add | solution.py:150
  336.5 1.4 collective-permute-start.10
  338.7 35.5 %collective-permute-done.10 = f32[2,3,16,1,4096]{4,2,3,1,0:T(8,128)} collective-permute-done((f32[2,3,16,1,4096]{4,2,3,1,0:T(8,128)}, f32[2,3,16,1,4096]{4,2,3,1,0:T(8,128)}, u32[]{:S(2)}, u32[]{:S(2)}) %collective-permute-start.10) | collective-permute-done | bytes 1572896 | tf_op jit(solution)/shard_map/ppermute | solution.py:18
  374.2 31.9 %collective-permute-done.11 = f32[2,3,16,1,4096]{4,2,3,1,0:T(8,128)S(1)} collective-permute-done((f32[2,3,16,1,4096]{4,2,3,1,0:T(8,128)S(1)}, f32[2,3,16,1,4096]{4,2,3,1,0:T(8,128)S(1)}, u32[]{:S(2)}, u32[]{:S(2)}) %collective-permute-start.11) | collective-permute-done | bytes 1572896 | tf_op jit(solution)/shard_map/ppermute | solution.py:18
  406.0 2.4 multiply_add_fusion
  410.6 12.0 %psum.7 = f32[16]{0:T(128)S(1)} all-reduce(f32[16]{0:T(128)S(1)} %get-tuple-element.32), channel_id=1, replica_groups=mesh['seq'=8,'chan'=4] {'seq'}, use_global_device_ids=true, to_apply=%region_1.2 | all-reduce | flops 16 | bytes 128 | tf_op jit(solution)/shard_map/psum | solution.py:215
  (51 shorter events, 11.6 us)
Async XLA Ops:
  4.4 38.5 %collective-permute-start = (f32[2,3,16,1,4096]{4,2,3,1,0:T(8,128)}, f32[2,3,16,1,4096]{4,2,3,1,0:T(8,128)}, u32[]{:S(2)}, u32[]{:S(2)}) collective-permute-start(f32[2,3,16,1,4096]{4,2,3,1,0:T(8,128)} %pad_maximum_fusion), channel_id=1, source_target_pairs={{0,16},{16,0},{4,20},{20,4},{8,24},{24,8},{12,28},{28,12},{1,17},{... | collective-permute-start | bytes 4718600 | tf_op jit(solution)/shard_map/ppermute | solution.py:18
  8.7 67.1 %collective-permute-start.1 = (f32[2,3,16,1,4096]{4,2,3,1,0:T(8,128)}, f32[2,3,16,1,4096]{4,2,3,1,0:T(8,128)}, u32[]{:S(2)}, u32[]{:S(2)}) collective-permute-start(f32[2,3,16,1,4096]{4,2,3,1,0:T(8,128)} %stack.65), channel_id=1, source_target_pairs={{0,16},{16,0},{4,20},{20,4},{8,24},{24,8},{12,28},{28,12},{1,17},{... | collective-permute-start | bytes 4718600 | tf_op jit(solution)/shard_map/ppermute | solution.py:18
  80.0 37.5 %collective-permute-start.2 = (f32[2,3,16,1,4096]{4,2,3,1,0:T(8,128)}, f32[2,3,16,1,4096]{4,2,3,1,0:T(8,128)S(1)}, u32[]{:S(2)}, u32[]{:S(2)}) collective-permute-start(f32[2,3,16,1,4096]{4,2,3,1,0:T(8,128)} %get-tuple-element.17), channel_id=1, source_target_pairs={{0,8},{8,0},{4,12},{12,4},{16,24},{24,16},{20,28},{28,20},{1,9},{9... | collective-permute-start | bytes 4718600 | tf_op jit(solution)/shard_map/ppermute | solution.py:18
  81.7 67.9 %collective-permute-start.3 = (f32[2,3,16,1,4096]{4,2,3,1,0:T(8,128)}, f32[2,3,16,1,4096]{4,2,3,1,0:T(8,128)}, u32[]{:S(2)}, u32[]{:S(2)}) collective-permute-start(f32[2,3,16,1,4096]{4,2,3,1,0:T(8,128)} %get-tuple-element.16), channel_id=1, source_target_pairs={{0,8},{8,0},{4,12},{12,4},{16,24},{24,16},{20,28},{28,20},{1,9},{9... | collective-permute-start | bytes 4718600 | tf_op jit(solution)/shard_map/ppermute | solution.py:18
  117.5 1.2 copy-start.3
  153.1 3.6 collective-permute-start.4
  153.1 5.8 %collective-permute-start.5 = (f32[2,3,16,1,4096]{4,2,3,1,0:T(8,128)S(1)}, f32[2,3,16,1,4096]{4,2,3,1,0:T(8,128)}, u32[]{:S(2)}, u32[]{:S(2)}) collective-permute-start(f32[2,3,16,1,4096]{4,2,3,1,0:T(8,128)S(1)} %get-tuple-element.15), channel_id=1, source_target_pairs={{0,4},{4,0},{8,12},{12,8},{16,20},{20,16},{24,28},{28,24},{1,5},{5... | collective-permute-start | bytes 4718600 | tf_op jit(solution)/shard_map/ppermute | solution.py:18
  168.9 16.5 %copy-start.4 = (f32[2,3,16,512,8]{3,4,2,1,0:T(8,128)}, f32[2,3,16,512,8]{3,4,2,1,0:T(8,128)S(1)}, u32[]{:S(2)}) copy-start(f32[2,3,16,512,8]{3,4,2,1,0:T(8,128)S(1)} %convolution_subtract_fusion) | copy-start | bytes 4718596
  170.6 14.8 %copy-start.5 = (f32[2,3,16,512,8]{3,4,2,1,0:T(8,128)}, f32[2,3,16,512,8]{3,4,2,1,0:T(8,128)S(1)}, u32[]{:S(2)}) copy-start(f32[2,3,16,512,8]{3,4,2,1,0:T(8,128)S(1)} %convolution_add_fusion) | copy-start | bytes 4718596
  252.6 3.6 copy-start.1
  252.6 3.6 copy-start.2
  252.6 3.6 collective-permute-start.6
  252.8 5.7 %collective-permute-start.7 = (f32[2,3,16,1,4096]{4,2,3,1,0:T(8,128)S(1)}, f32[2,3,16,1,4096]{4,2,3,1,0:T(8,128)}, u32[]{:S(2)}, u32[]{:S(2)}) collective-permute-start(f32[2,3,16,1,4096]{4,2,3,1,0:T(8,128)S(1)} %get-tuple-element.19), channel_id=1, source_target_pairs={{0,4},{4,0},{8,12},{12,8},{16,20},{20,16},{24,28},{28,24},{1,5},{5... | collective-permute-start | bytes 4718600 | tf_op jit(solution)/shard_map/ppermute | solution.py:18
  261.9 37.4 %copy-start = (f32[2,3,16,1,4096]{4,2,3,1,0:T(8,128)}, f32[2,3,16,1,4096]{4,2,3,1,0:T(8,128)S(1)}, u32[]{:S(2)}) copy-start(f32[2,3,16,1,4096]{4,2,3,1,0:T(8,128)S(1)} %get-tuple-element.13) | copy-start | bytes 4718596
  261.9 37.4 %collective-permute-start.8 = (f32[2,3,16,1,4096]{4,2,3,1,0:T(8,128)S(1)}, f32[2,3,16,1,4096]{4,2,3,1,0:T(8,128)}, u32[]{:S(2)}, u32[]{:S(2)}) collective-permute-start(f32[2,3,16,1,4096]{4,2,3,1,0:T(8,128)S(1)} %get-tuple-element.12), channel_id=1, source_target_pairs={{0,8},{8,0},{4,12},{12,4},{16,24},{24,16},{20,28},{28,20},{1,9},{9... | collective-permute-start | bytes 4718600 | tf_op jit(solution)/shard_map/ppermute | solution.py:18
  263.4 68.9 %collective-permute-start.9 = (f32[2,3,16,1,4096]{4,2,3,1,0:T(8,128)S(1)}, f32[2,3,16,1,4096]{4,2,3,1,0:T(8,128)}, u32[]{:S(2)}, u32[]{:S(2)}) collective-permute-start(f32[2,3,16,1,4096]{4,2,3,1,0:T(8,128)S(1)} %get-tuple-element.13), channel_id=1, source_target_pairs={{0,8},{8,0},{4,12},{12,4},{16,24},{24,16},{20,28},{28,20},{1,9},{9... | collective-permute-start | bytes 4718600 | tf_op jit(solution)/shard_map/ppermute | solution.py:18
  336.5 37.6 %collective-permute-start.10 = (f32[2,3,16,1,4096]{4,2,3,1,0:T(8,128)}, f32[2,3,16,1,4096]{4,2,3,1,0:T(8,128)}, u32[]{:S(2)}, u32[]{:S(2)}) collective-permute-start(f32[2,3,16,1,4096]{4,2,3,1,0:T(8,128)} %get-tuple-element.10), channel_id=1, source_target_pairs={{0,16},{16,0},{4,20},{20,4},{8,24},{24,8},{12,28},{28,12},{1,17},{... | collective-permute-start | bytes 4718600 | tf_op jit(solution)/shard_map/ppermute | solution.py:18
  337.9 68.1 %collective-permute-start.11 = (f32[2,3,16,1,4096]{4,2,3,1,0:T(8,128)S(1)}, f32[2,3,16,1,4096]{4,2,3,1,0:T(8,128)S(1)}, u32[]{:S(2)}, u32[]{:S(2)}) collective-permute-start(f32[2,3,16,1,4096]{4,2,3,1,0:T(8,128)S(1)} %get-tuple-element.11), channel_id=1, source_target_pairs={{0,16},{16,0},{4,20},{20,4},{8,24},{24,8},{12,28},{28,12},{1,17},{... | collective-permute-start | bytes 4718600 | tf_op jit(solution)/shard_map/ppermute | solution.py:18
  408.4 1.1 copy-start.6
  408.4 1.1 copy-start.7
  408.5 1.1 copy-start.8
  408.5 1.1 copy-start.9
  408.5 1.1 copy-start.10
where the time goes:
time: 427 us; the launch traced here: 423 us
  waiting for transfers between devices  277 us (65%)
  matrix products  76 us (18%)
  other arithmetic  31.5 us (7%)
  local copies, waits for them, and re-layouts  14.3 us (3%)
  blocking collectives  12 us (3%)
  starting transfers between devices  10.3 us (2%)
    ppermute x12, waiting for transfers between devices, from_partner(): return lax.ppermute(block, axis, route)  277 us
    dot_general x4, matrix products, complex_product(): imag_real = jnp.einsum(pattern, left_im, right_re, precision=highest)  22.6 us
    dot_general x4, matrix products, complex_product(): real_imag = jnp.einsum(pattern, left_re, right_im, precision=highest)  19.1 us
    dot_general x4, matrix products, complex_product(): imag_imag = jnp.einsum(pattern, left_im, right_im, precision=highest)  17.8 us
    dot_general x4, matrix products, complex_product(): real_real = jnp.einsum(pattern, left_re, right_re, precision=highest)  16.5 us
    psum x1, blocking collectives, local(): skip_sum = lax.psum(skip_part, 'seq')  12 us
    ppermute x12, starting transfers between devices, from_partner(): return lax.ppermute(block, axis, route)  10.3 us
    add x3, other arithmetic, to_signal(): real_part = base_re + flip_sign * turned_re  10.1 us
  transfers between devices with their start and end apart: 12, of which 12 were waited for; matrix products, arithmetic and copies ran while one was open for 1% of the time, Pallas kernels for 0%

commit v1 on v0

--- a/solution.py
+++ b/solution.py
@@ -1,8 +1,13 @@
+import functools
 import math
 
 import jax
 import jax.numpy as jnp
+import ml_dtypes
+import numpy as np
 from jax import lax
+from jax.experimental import pallas as pl
+from jax.experimental.pallas import tpu as pltpu
 from jax.sharding import PartitionSpec as P
 
 highest = lax.Precision.HIGHEST
@@ -154,7 +159,7 @@
     return combined / padded_len
 
 
-def local(queries, key_proj, value_proj, cotangent, filter_taps, skip_gain):
+def local_butterfly(queries, key_proj, value_proj, cotangent, filter_taps, skip_gain):
     seq_count = lax.axis_size("seq")
     seq_index = lax.axis_index("seq")
     tok_local = queries.shape[1]
@@ -216,6 +221,245 @@
     return (grad_query, grad_key, grad_value, grad_filter, skip_sum * norm_scale)
 
 
+LANES = 128
+
+
+def halves(table):
+    high = table.astype(np.float32).astype(ml_dtypes.bfloat16)
+    low = (table - high.astype(np.float64)).astype(np.float32).astype(ml_dtypes.bfloat16)
+    return jnp.asarray(high), jnp.asarray(low)
+
+
+def transform_tables(rows):
+    total = rows * LANES
+    quarter = np.arange(rows) + 0.25
+    outer = 2.0 * np.pi / rows * np.outer(quarter, np.arange(rows))
+    turn = 2.0 * np.pi / total * np.outer(quarter, np.arange(LANES))
+    inner = 2.0 * np.pi / LANES * np.outer(np.arange(LANES), np.arange(LANES))
+    first = np.concatenate([np.cos(outer), -np.sin(outer)], axis=0)
+    second = np.block([[np.cos(inner), -np.sin(inner)], [np.sin(inner), np.cos(inner)]])
+    second_back = np.block([[np.cos(inner), np.sin(inner)], [-np.sin(inner), np.cos(inner)]])
+    first_back = np.concatenate([np.cos(outer.T), -np.sin(outer.T)], axis=1) / total
+    return (
+        *halves(first),
+        *halves(second),
+        *halves(second_back),
+        *halves(first_back),
+        jnp.asarray(np.cos(turn).astype(np.float32)),
+        jnp.asarray(np.sin(turn).astype(np.float32)),
+    )
+
+
+def split(value):
+    high = value.astype(jnp.bfloat16)
+    low = (value - high.astype(jnp.float32)).astype(jnp.bfloat16)
+    return high, low
+
+
+def dot(left, right):
+    return jnp.dot(left, right, preferred_element_type=jnp.float32)
+
+
+def channel_kernel(
+    count,
+    query_ref, key_ref, value_ref, cot_ref, taps_ref, gain_ref,
+    first_h, first_l, second_h, second_l, back2_h, back2_l, back1_h, back1_l, cos_ref, sin_ref,
+    gq_ref, gk_ref, gv_ref, gf_ref, skip_ref,
+    out_box, in_box, res_box, got_box, sum_box, sum_got,
+    send_in, recv_in, send_res, recv_res, send_sum, recv_sum,
+):
+    me = lax.axis_index("seq")
+    chans, tok_local = query_ref.shape
+    per = chans // count
+    part = tok_local // LANES
+    rows = part * count
+    norm_scale = 1.0 / math.sqrt(rows * LANES)
+
+    def peer_of(step):
+        return me ^ step
+
+    barrier = pltpu.get_barrier_semaphore()
+    for step in range(1, count):
+        pl.semaphore_signal(barrier, inc=1, device_id={"seq": peer_of(step)}, device_id_type=pl.DeviceIdType.MESH)
+
+    inputs = (query_ref, key_ref, value_ref, cot_ref, taps_ref)
+    for slot, ref in enumerate(inputs):
+        pieces = jnp.stack([ref[:, r * LANES : (r + 1) * LANES].astype(jnp.float32) for r in range(part)])
+        turned = jnp.swapaxes(pieces, 0, 1).astype(jnp.bfloat16)
+        out_box[:, :, slot] = turned.reshape(count, per, part, LANES)
+
+    pl.semaphore_wait(barrier, count - 1)
+
+    def send_copy(chan, step):
+        peer = peer_of(step)
+        return pltpu.make_async_remote_copy(
+            src_ref=out_box.at[peer, chan],
+            dst_ref=in_box.at[chan, me],
+            send_sem=send_in.at[chan, step],
+            recv_sem=recv_in.at[chan, step],
+            device_id={"seq": peer},
+            device_id_type=pl.DeviceIdType.MESH,
+        )
+
+    def result_copy(chan, step):
+        peer = peer_of(step)
+        return pltpu.make_async_remote_copy(
+            src_ref=res_box.at[chan, peer],
+            dst_ref=got_box.at[me, chan],
+            send_sem=send_res.at[chan, step],
+            recv_sem=recv_res.at[chan, step],
+            device_id={"seq": peer},
+            device_id_type=pl.DeviceIdType.MESH,
+        )
+
+    def sum_copy(step):
+        peer = peer_of(step)
+        return pltpu.make_async_remote_copy(
+            src_ref=sum_box,
+            dst_ref=sum_got.at[me],
+            send_sem=send_sum.at[step],
+            recv_sem=recv_sum.at[step],
+            device_id={"seq": peer},
+            device_id_type=pl.DeviceIdType.MESH,
+        )
+
+    for chan in range(per):
+        for step in reversed(range(1, count)):
+            send_copy(chan, step).start()
+    for chan in range(per):
+        in_box[chan, me] = out_box[me, chan]
+
+    def one_channel(chan, carry):
+        for step in range(1, count):
+            send_copy(chan, step).wait_recv()
+        arrived = [in_box[chan, :, slot].reshape(rows, LANES) for slot in range(5)]
+        query_f, key_f, value_f, cot_f = [a.astype(jnp.float32) for a in arrived[:4]]
+        taps = arrived[4]
+        mixed = key_f * value_f
+        gated = cot_f * query_f
+        mixed_h, mixed_l = split(mixed)
+        gated_h, gated_l = split(gated)
+
+        high = jnp.concatenate([mixed_h, gated_h], axis=1)
+        low = jnp.concatenate([mixed_l, gated_l], axis=1)
+        pair = dot(first_h[...], high) + dot(first_h[...], low) + dot(first_l[...], high)
+        both = dot(jnp.concatenate([first_h[...], first_l[...]], axis=0), taps)
+        tap_out = both[: 2 * rows] + both[2 * rows :]
+        cosine, sine = cos_ref[...], sin_ref[...]
+        turned = []
+        for block in (pair[:, :LANES], pair[:, LANES:], tap_out):
+            real, imag = block[:rows], block[rows:]
+            turned.append(jnp.concatenate([real * cosine + imag * sine, imag * cosine - real * sine], axis=1))
+        work_h, work_l = split(jnp.concatenate(turned, axis=0))
+        spec = dot(work_h, second_h[...]) + dot(work_l, second_h[...]) + dot(work_h, second_l[...])
+        mix_re, mix_im = spec[:rows, :LANES], spec[:rows, LANES:]
+        grad_re, grad_im = spec[rows : 2 * rows, :LANES], spec[rows : 2 * rows, LANES:]
+        ker_re, ker_im = spec[2 * rows :, :LANES], spec[2 * rows :, LANES:]
+        prods = jnp.concatenate(
+            [
+                jnp.concatenate([ker_re * mix_re - ker_im * mix_im, ker_re * mix_im + ker_im * mix_re], axis=1),
+                jnp.concatenate([ker_re * grad_re + ker_im * grad_im, ker_re * grad_im - ker_im * grad_re], axis=1),
+                jnp.concatenate([grad_re * mix_re + grad_im * mix_im, grad_im * mix_re - grad_re * mix_im], axis=1),
+            ],
+            axis=0,
+        )
+        prod_h, prod_l = split(prods)
+        work = dot(prod_h, back2_h[...]) + dot(prod_l, back2_h[...]) + dot(prod_h, back2_l[...])
+        turned = []
+        for block in range(3):
+            real = work[block * rows : (block + 1) * rows, :LANES]
+            imag = work[block * rows : (block + 1) * rows, LANES:]
+            turned.append(jnp.concatenate([real * cosine - imag * sine, imag * cosine + real * sine], axis=0))
+        work_h, work_l = split(jnp.concatenate(turned, axis=1))
+        result = dot(back1_h[...], work_h) + dot(back1_h[...], work_l) + dot(back1_l[...], work_h)
+        convolved, carried, lag_grad = [result[:, i * LANES : (i + 1) * LANES] for i in range(3)]
+
+        gain = gain_ref[me * per + chan]
+        grad_mixed = carried + gain * gated
+        finals = (
+            cot_f * (convolved + gain * mixed),
+            grad_mixed * value_f,
+            grad_mixed * key_f,
+            lag_grad * norm_scale,
+        )
+        for slot, value in enumerate(finals):
+            res_box[chan, :, slot] = value.astype(jnp.bfloat16).reshape(count, part, LANES)
+        for step in reversed(range(1, count)):
+            result_copy(chan, step).start()
+        total = jnp.sum(jnp.sum(gated * mixed, axis=0, keepdims=True), axis=1, keepdims=True) * norm_scale
+        sum_box[chan] = jnp.broadcast_to(total, (8, LANES))
+        return carry
+
+    lax.fori_loop(0, per, one_channel, 0)
+
+    for step in range(1, count):
+        sum_copy(step).start()
+    for chan in range(per):
+        got_box[me, chan] = res_box[chan, me]
+    sum_got[me] = sum_box[...]
+    for chan in range(per):
+        for step in range(1, count):
+            send_copy(chan, step).wait_send()
+    for step in range(1, count):
+        sum_copy(step).wait()
+    for chan in range(per):
+        for step in range(1, count):
+            result_copy(chan, step).wait()
+
+    for slot, ref in enumerate((gq_ref, gk_ref, gv_ref, gf_ref)):
+        pieces = got_box[:, :, slot].reshape(chans, part, LANES).astype(jnp.float32)
+        turned = jnp.swapaxes(pieces, 0, 1).astype(jnp.bfloat16)
+        for r in range(part):
+            ref[:, r * LANES : (r + 1) * LANES] = turned[r]
+    skip_ref[...] = sum_got[...].reshape(chans, 8, LANES)[:, 0, :]
+
+
+def local_channels(queries, key_proj, value_proj, cotangent, filter_taps, skip_gain):
+    count = lax.axis_size("seq")
+    chans, tok_local = queries.shape
+    per = chans // count
+    part = tok_local // LANES
+    rows = part * count
+    tables = transform_tables(rows)
+    vmem = pl.BlockSpec(memory_space=pltpu.VMEM)
+    smem = pl.BlockSpec(memory_space=pltpu.SMEM)
+    block = jax.ShapeDtypeStruct((chans, tok_local), jnp.bfloat16)
+    dma = pltpu.SemaphoreType.DMA
+    *grads, skips = pl.pallas_call(
+        functools.partial(channel_kernel, count),
+        out_shape=[block] * 4 + [jax.ShapeDtypeStruct((chans, LANES), jnp.float32)],
+        in_specs=[vmem] * 5 + [smem] + [vmem] * 10,
+        out_specs=[vmem] * 5,
+        scratch_shapes=[
+            pltpu.VMEM((count, per, 5, part, LANES), jnp.bfloat16),
+            pltpu.VMEM((per, count, 5, part, LANES), jnp.bfloat16),
+            pltpu.VMEM((per, count, 4, part, LANES), jnp.bfloat16),
+            pltpu.VMEM((count, per, 4, part, LANES), jnp.bfloat16),
+            pltpu.VMEM((per, 8, LANES), jnp.float32),
+            pltpu.VMEM((count, per, 8, LANES), jnp.float32),
+            dma((per, count)),
+            dma((per, count)),
+            dma((per, count)),
+            dma((per, count)),
+            dma((count,)),
+            dma((count,)),
+        ],
+        compiler_params=pltpu.CompilerParams(
+            collective_id=0, has_side_effects=True, vmem_limit_bytes=48 * 1024 * 1024
+        ),
+    )(queries, key_proj, value_proj, cotangent, filter_taps, skip_gain, *tables)
+    return (*grads, skips[:, 0])
+
+
+def local(*arguments):
+    count = lax.axis_size("seq")
+    chans, tok_local = arguments[0].shape
+    whole_channels = chans % count == 0 and count & (count - 1) == 0
+    if whole_channels and count > 1 and tok_local % (16 * LANES) == 0 and count * tok_local <= 65536:
+        return local_channels(*arguments)
+    return local_butterfly(*arguments)
+
+
 def solution(mesh):
     return jax.shard_map(
         local,

time: 427 us -> 40.8 us (0.10)
  waiting for transfers between devices: 277 us -> 0 us
  matrix products: 76 us -> 0 us
  other arithmetic: 31.5 us -> 0 us
  Pallas kernels: 0 us -> 22 us
  blocking collectives: 12 us -> 0 us
  starting transfers between devices: 10.3 us -> 0 us
    ppermute x12 -> x0, waiting for transfers between devices: 277 us -> none  [from_partner(): return lax.ppermute(block, axis, route)]
    dot_general x16 -> x0, matrix products: 76 us -> none  [the longest x4 22.6 us: complex_product(): imag_real = jnp.einsum(pattern, left_im, right_re, precision=highest)]
    pallas_call x0 -> x1, Pallas kernels: none -> 22 us  [local_channels(): pl.pallas_call(functools.partial(channel_kernel, count), out_shape=[block...]
    add x7 -> x0, other arithmetic: 14.9 us -> none  [the longest x3 10.1 us: to_signal(): real_part = base_re + flip_sign * turned_re]
    psum x1 -> x0, blocking collectives: 12 us -> none  [local(): skip_sum = lax.psum(skip_part, 'seq')]
    unnamed x30 -> x36, local copies, waits for them, and re-layouts: 5.29 us -> 17 us
    ppermute x12 -> x0, starting transfers between devices: 10.3 us -> none  [from_partner(): return lax.ppermute(block, axis, route)]
    sub x4 -> x0, other arithmetic: 8.66 us -> none  [the longest x3 8.51 us: rotate(): real_in * cosine - imag_in * sine_val]
  transfers between devices with their start and end apart: 12 -> 0, of which waited for: 12 -> 0; matrix products, arithmetic and copies ran while one was open for 1% -> 0% of each run, Pallas kernels for 0% -> 0%
where the time goes in v1:
time: 40.8 us; the launch traced here: 40.3 us
  Pallas kernels  22 us (54%)
  local copies, waits for them, and re-layouts  17.6 us (43%)
  between operations  0.67 us (2%)
    pallas_call x1, Pallas kernels, local_channels(): pl.pallas_call(functools.partial(channel_kernel, count), out_shape=[block...  22 us
    unnamed x36, local copies, waits for them, and re-layouts  17 us

profile of v1, /device:TPU:0, one launch (start us, length us, event | category | flops | bytes accessed | tf_op | source)
XLA Modules:
  0.0 40.3 jit_solution(5398606068609958240)
XLA Ops:
  0.6 0.0 copy-start
  0.6 0.9 %copy-done = bf16[256,512]{1,0:T(8,128)(2,1)S(1)} copy-done((bf16[256,512]{1,0:T(8,128)(2,1)S(1)}, bf16[256,512]{1,0:T(8,128)(2,1)}, u32[]{:S(2)}) %copy-start) | copy-done | bytes 262168
  1.6 0.0 copy-start.1
  1.6 0.9 %copy-done.1 = bf16[256,512]{1,0:T(8,128)(2,1)S(1)} copy-done((bf16[256,512]{1,0:T(8,128)(2,1)S(1)}, bf16[256,512]{1,0:T(8,128)(2,1)}, u32[]{:S(2)}) %copy-start.1) | copy-done | bytes 262168
  2.5 0.0 copy-start.2
  2.5 0.9 %copy-done.2 = bf16[512,256]{1,0:T(8,128)(2,1)S(1)} copy-done((bf16[512,256]{1,0:T(8,128)(2,1)S(1)}, bf16[512,256]{1,0:T(8,128)(2,1)}, u32[]{:S(2)}) %copy-start.2) | copy-done | bytes 262168
  3.5 0.0 copy-start.3
  3.5 0.9 %copy-done.3 = bf16[512,256]{1,0:T(8,128)(2,1)S(1)} copy-done((bf16[512,256]{1,0:T(8,128)(2,1)S(1)}, bf16[512,256]{1,0:T(8,128)(2,1)}, u32[]{:S(2)}) %copy-start.3) | copy-done | bytes 262168
  4.4 0.0 copy-start.4
  4.4 0.9 %copy-done.4 = bf16[16,4096]{1,0:T(8,128)(2,1)S(1)} copy-done((bf16[16,4096]{1,0:T(8,128)(2,1)S(1)}, bf16[16,4096]{1,0:T(8,128)(2,1)}, u32[]{:S(2)}) %copy-start.4) | copy-done | bytes 131096
  5.3 0.0 copy-start.5
  5.3 0.9 %copy-done.5 = bf16[16,4096]{1,0:T(8,128)(2,1)S(1)} copy-done((bf16[16,4096]{1,0:T(8,128)(2,1)S(1)}, bf16[16,4096]{1,0:T(8,128)(2,1)}, u32[]{:S(2)}) %copy-start.5) | copy-done | bytes 131096
  6.2 0.0 copy-start.6
  6.2 0.9 %copy-done.6 = bf16[16,4096]{1,0:T(8,128)(2,1)S(1)} copy-done((bf16[16,4096]{1,0:T(8,128)(2,1)S(1)}, bf16[16,4096]{1,0:T(8,128)(2,1)}, u32[]{:S(2)}) %copy-start.6) | copy-done | bytes 131096
  7.2 0.0 copy-start.7
  7.2 0.9 %copy-done.7 = bf16[16,4096]{1,0:T(8,128)(2,1)S(1)} copy-done((bf16[16,4096]{1,0:T(8,128)(2,1)S(1)}, bf16[16,4096]{1,0:T(8,128)(2,1)}, u32[]{:S(2)}) %copy-start.7) | copy-done | bytes 131096
  8.1 0.0 copy-start.8
  8.1 0.9 %copy-done.8 = bf16[16,4096]{1,0:T(8,128)(2,1)S(1)} copy-done((bf16[16,4096]{1,0:T(8,128)(2,1)S(1)}, bf16[16,4096]{1,0:T(8,128)(2,1)}, u32[]{:S(2)}) %copy-start.8) | copy-done | bytes 131096
  9.0 0.0 copy-start.9
  9.0 0.9 %copy-done.9 = f32[256,128]{1,0:T(8,128)S(1)} copy-done((f32[256,128]{1,0:T(8,128)S(1)}, f32[256,128]{1,0:T(8,128)}, u32[]{:S(2)}) %copy-start.9) | copy-done | bytes 131096
  9.9 0.0 copy-start.10
  9.9 0.9 %copy-done.10 = f32[256,128]{1,0:T(8,128)S(1)} copy-done((f32[256,128]{1,0:T(8,128)S(1)}, f32[256,128]{1,0:T(8,128)}, u32[]{:S(2)}) %copy-start.10) | copy-done | bytes 131096
  10.8 0.0 copy-start.11
  10.8 0.9 %copy-done.11 = bf16[256,256]{1,0:T(8,128)(2,1)S(1)} copy-done((bf16[256,256]{1,0:T(8,128)(2,1)S(1)}, bf16[256,256]{1,0:T(8,128)(2,1)}, u32[]{:S(2)}) %copy-start.11) | copy-done | bytes 131096
  11.7 0.0 copy-start.12
  11.7 0.9 %copy-done.12 = bf16[256,256]{1,0:T(8,128)(2,1)S(1)} copy-done((bf16[256,256]{1,0:T(8,128)(2,1)S(1)}, bf16[256,256]{1,0:T(8,128)(2,1)}, u32[]{:S(2)}) %copy-start.12) | copy-done | bytes 131096
  12.6 0.0 copy-start.13
  12.6 0.9 %copy-done.13 = bf16[256,256]{1,0:T(8,128)(2,1)S(1)} copy-done((bf16[256,256]{1,0:T(8,128)(2,1)S(1)}, bf16[256,256]{1,0:T(8,128)(2,1)}, u32[]{:S(2)}) %copy-start.13) | copy-done | bytes 131096
  13.5 0.0 copy-start.14
  13.5 0.9 %copy-done.14 = bf16[256,256]{1,0:T(8,128)(2,1)S(1)} copy-done((bf16[256,256]{1,0:T(8,128)(2,1)S(1)}, bf16[256,256]{1,0:T(8,128)(2,1)}, u32[]{:S(2)}) %copy-start.14) | copy-done | bytes 131096
  14.4 0.0 copy-start.15
  14.4 0.7 %copy-done.15 = f32[16]{0:T(128)S(1)} copy-done((f32[16]{0:T(128)S(1)}, f32[16]{0:T(128)}, u32[]{:S(2)}) %copy-start.15) | copy-done | bytes 88
  15.0 22.0 %shard_map.191 = (bf16[16,4096]{1,0:T(8,128)(2,1)S(1)}, bf16[16,4096]{1,0:T(8,128)(2,1)S(1)}, bf16[16,4096]{1,0:T(8,128)(2,1)S(1)}, bf16[16,4096]{1,0:T(8,128)(2,1)S(1)}, f32[16,128]{1,0:T(8,128)S(1)}) custom-call(bf16[16,4096]{1,0:T(8,128)(2,1)S(1)} %copy-done.4, bf16[16,4096]{1,0:T(8,128)(2,1)S(1)} %copy-done.5, bf16[16,4096]{1,0:T(8,128)(2,1)S(1)} %copy-done.6, ...), custom_call_target="tpu_custom_call" | custom-call | tf_op jit(solution)/shard_map/pallas_call | solution.py:428
  37.1 0.6 %slice_reduce_fusion = f32[16]{0:T(128)} fusion(f32[16,128]{1,0:T(8,128)S(1)} %get-tuple-element.14), kind=kLoop, calls=%fused_computation | loop fusion | bytes 128 | tf_op jit(solution)/shard_map/slice | solution.py:451
  37.7 0.7 %copy.25 = bf16[16,4096]{1,0:T(8,128)(2,1)} copy(bf16[16,4096]{1,0:T(8,128)(2,1)S(1)} %get-tuple-element.20) | data formatting | bytes 262144
  38.3 0.7 %copy.26 = bf16[16,4096]{1,0:T(8,128)(2,1)} copy(bf16[16,4096]{1,0:T(8,128)(2,1)S(1)} %get-tuple-element.21) | data formatting | bytes 262144
  39.0 0.7 %copy.27 = bf16[16,4096]{1,0:T(8,128)(2,1)} copy(bf16[16,4096]{1,0:T(8,128)(2,1)S(1)} %get-tuple-element.22) | data formatting | bytes 262144
  39.7 0.7 %copy.28 = bf16[16,4096]{1,0:T(8,128)(2,1)} copy(bf16[16,4096]{1,0:T(8,128)(2,1)S(1)} %get-tuple-element.23) | data formatting | bytes 262144
Async XLA Ops:
  0.6 1.0 %copy-start = (bf16[256,512]{1,0:T(8,128)(2,1)S(1)}, bf16[256,512]{1,0:T(8,128)(2,1)}, u32[]{:S(2)}) copy-start(bf16[256,512]{1,0:T(8,128)(2,1)} %constant.27.clone.back1_l) | copy-start | bytes 786436
  1.6 0.9 %copy-start.1 = (bf16[256,512]{1,0:T(8,128)(2,1)S(1)}, bf16[256,512]{1,0:T(8,128)(2,1)}, u32[]{:S(2)}) copy-start(bf16[256,512]{1,0:T(8,128)(2,1)} %constant.26.clone.back1_h) | copy-start | bytes 786436
  2.5 0.9 %copy-start.2 = (bf16[512,256]{1,0:T(8,128)(2,1)S(1)}, bf16[512,256]{1,0:T(8,128)(2,1)}, u32[]{:S(2)}) copy-start(bf16[512,256]{1,0:T(8,128)(2,1)} %constant.21.clone.first_l) | copy-start | bytes 786436
  3.5 0.9 %copy-start.3 = (bf16[512,256]{1,0:T(8,128)(2,1)S(1)}, bf16[512,256]{1,0:T(8,128)(2,1)}, u32[]{:S(2)}) copy-start(bf16[512,256]{1,0:T(8,128)(2,1)} %constant.20.clone.first_h) | copy-start | bytes 786436
  4.4 0.9 %copy-start.4 = (bf16[16,4096]{1,0:T(8,128)(2,1)S(1)}, bf16[16,4096]{1,0:T(8,128)(2,1)}, u32[]{:S(2)}) copy-start(bf16[16,4096]{1,0:T(8,128)(2,1)} %query_ref.1) | copy-start | bytes 393220
  5.3 0.9 %copy-start.5 = (bf16[16,4096]{1,0:T(8,128)(2,1)S(1)}, bf16[16,4096]{1,0:T(8,128)(2,1)}, u32[]{:S(2)}) copy-start(bf16[16,4096]{1,0:T(8,128)(2,1)} %key_ref.1) | copy-start | bytes 393220
  6.2 0.9 %copy-start.6 = (bf16[16,4096]{1,0:T(8,128)(2,1)S(1)}, bf16[16,4096]{1,0:T(8,128)(2,1)}, u32[]{:S(2)}) copy-start(bf16[16,4096]{1,0:T(8,128)(2,1)} %value_ref.1) | copy-start | bytes 393220
  7.2 0.9 %copy-start.7 = (bf16[16,4096]{1,0:T(8,128)(2,1)S(1)}, bf16[16,4096]{1,0:T(8,128)(2,1)}, u32[]{:S(2)}) copy-start(bf16[16,4096]{1,0:T(8,128)(2,1)} %cot_ref.1) | copy-start | bytes 393220
  8.1 0.9 %copy-start.8 = (bf16[16,4096]{1,0:T(8,128)(2,1)S(1)}, bf16[16,4096]{1,0:T(8,128)(2,1)}, u32[]{:S(2)}) copy-start(bf16[16,4096]{1,0:T(8,128)(2,1)} %taps_ref.1) | copy-start | bytes 393220
  9.0 0.9 %copy-start.9 = (f32[256,128]{1,0:T(8,128)S(1)}, f32[256,128]{1,0:T(8,128)}, u32[]{:S(2)}) copy-start(f32[256,128]{1,0:T(8,128)} %constant.29.clone.sin_ref) | copy-start | bytes 393220
  9.9 0.9 %copy-start.10 = (f32[256,128]{1,0:T(8,128)S(1)}, f32[256,128]{1,0:T(8,128)}, u32[]{:S(2)}) copy-start(f32[256,128]{1,0:T(8,128)} %constant.28.clone.cos_ref) | copy-start | bytes 393220
  10.8 0.9 %copy-start.11 = (bf16[256,256]{1,0:T(8,128)(2,1)S(1)}, bf16[256,256]{1,0:T(8,128)(2,1)}, u32[]{:S(2)}) copy-start(bf16[256,256]{1,0:T(8,128)(2,1)} %constant.25.clone.back2_l) | copy-start | bytes 393220
  11.7 0.9 %copy-start.12 = (bf16[256,256]{1,0:T(8,128)(2,1)S(1)}, bf16[256,256]{1,0:T(8,128)(2,1)}, u32[]{:S(2)}) copy-start(bf16[256,256]{1,0:T(8,128)(2,1)} %constant.24.clone.back2_h) | copy-start | bytes 393220
  12.6 0.9 %copy-start.13 = (bf16[256,256]{1,0:T(8,128)(2,1)S(1)}, bf16[256,256]{1,0:T(8,128)(2,1)}, u32[]{:S(2)}) copy-start(bf16[256,256]{1,0:T(8,128)(2,1)} %constant.23.clone.second_l) | copy-start | bytes 393220
  13.5 0.9 %copy-start.14 = (bf16[256,256]{1,0:T(8,128)(2,1)S(1)}, bf16[256,256]{1,0:T(8,128)(2,1)}, u32[]{:S(2)}) copy-start(bf16[256,256]{1,0:T(8,128)(2,1)} %constant.22.clone.second_h) | copy-start | bytes 393220
  14.4 0.7 %copy-start.15 = (f32[16]{0:T(128)S(1)}, f32[16]{0:T(128)}, u32[]{:S(2)}) copy-start(f32[16]{0:T(128)} %gain_ref.1) | copy-start | bytes 196

commit v2 on v1

--- a/solution.py
+++ b/solution.py
@@ -262,19 +262,28 @@
 
 def channel_kernel(
     count,
-    query_ref, key_ref, value_ref, cot_ref, taps_ref, gain_ref,
-    first_h, first_l, second_h, second_l, back2_h, back2_l, back1_h, back1_l, cos_ref, sin_ref,
-    gq_ref, gk_ref, gv_ref, gf_ref, skip_ref,
-    out_box, in_box, res_box, got_box, sum_box, sum_got,
-    send_in, recv_in, send_res, recv_res, send_sum, recv_sum,
+    *refs,
 ):
+    args, gain_ref, tables, refs = refs[:5], refs[5], refs[6:16], refs[16:]
+    gq_ref, gk_ref, gv_ref, gf_ref, skip_ref = refs[:5]
+    arg_vmem, table_vmem, refs = refs[5:10], refs[10:20], refs[20:]
+    out_box, in_box, res_box, got_box, sum_box, sum_got = refs[:6]
+    send_in, recv_in, send_res, recv_res, send_sum, recv_sum, load_sem = refs[6:]
+    first_h, first_l, second_h, second_l, back2_h, back2_l, back1_h, back1_l, cos_ref, sin_ref = table_vmem
     me = lax.axis_index("seq")
-    chans, tok_local = query_ref.shape
+    chans, tok_local = args[0].shape
     per = chans // count
     part = tok_local // LANES
     rows = part * count
     norm_scale = 1.0 / math.sqrt(rows * LANES)
 
+    loads = [
+        pltpu.make_async_copy(source, target, load_sem.at[i])
+        for i, (source, target) in enumerate(zip(args + tables, arg_vmem + table_vmem))
+    ]
+    for load in loads[:5]:
+        load.start()
+
     def peer_of(step):
         return me ^ step
 
@@ -282,8 +291,10 @@
     for step in range(1, count):
         pl.semaphore_signal(barrier, inc=1, device_id={"seq": peer_of(step)}, device_id_type=pl.DeviceIdType.MESH)
 
-    inputs = (query_ref, key_ref, value_ref, cot_ref, taps_ref)
-    for slot, ref in enumerate(inputs):
+    for load in loads[5:]:
+        load.start()
+    for slot, ref in enumerate(arg_vmem):
+        loads[slot].wait()
         pieces = jnp.stack([ref[:, r * LANES : (r + 1) * LANES].astype(jnp.float32) for r in range(part)])
         turned = jnp.swapaxes(pieces, 0, 1).astype(jnp.bfloat16)
         out_box[:, :, slot] = turned.reshape(count, per, part, LANES)
@@ -328,6 +339,9 @@
             send_copy(chan, step).start()
     for chan in range(per):
         in_box[chan, me] = out_box[me, chan]
+
+    for load in loads[5:]:
+        load.wait()
 
     def one_channel(chan, carry):
         for step in range(1, count):
@@ -422,15 +436,18 @@
     rows = part * count
     tables = transform_tables(rows)
     vmem = pl.BlockSpec(memory_space=pltpu.VMEM)
+    hbm = pl.BlockSpec(memory_space=pltpu.HBM)
     smem = pl.BlockSpec(memory_space=pltpu.SMEM)
     block = jax.ShapeDtypeStruct((chans, tok_local), jnp.bfloat16)
     dma = pltpu.SemaphoreType.DMA
     *grads, skips = pl.pallas_call(
         functools.partial(channel_kernel, count),
         out_shape=[block] * 4 + [jax.ShapeDtypeStruct((chans, LANES), jnp.float32)],
-        in_specs=[vmem] * 5 + [smem] + [vmem] * 10,
+        in_specs=[hbm] * 5 + [smem] + [hbm] * 10,
         out_specs=[vmem] * 5,
         scratch_shapes=[
+            *[pltpu.VMEM((chans, tok_local), jnp.bfloat16) for _ in range(5)],
+            *[pltpu.VMEM(table.shape, table.dtype) for table in tables],
             pltpu.VMEM((count, per, 5, part, LANES), jnp.bfloat16),
             pltpu.VMEM((per, count, 5, part, LANES), jnp.bfloat16),
             pltpu.VMEM((per, count, 4, part, LANES), jnp.bfloat16),
@@ -443,6 +460,7 @@
             dma((per, count)),
             dma((count,)),
             dma((count,)),
+            dma((15,)),
         ],
         compiler_params=pltpu.CompilerParams(
             collective_id=0, has_side_effects=True, vmem_limit_bytes=48 * 1024 * 1024

time: 40.8 us -> 41.9 us (1.027)
  Pallas kernels: 22 us -> 23.1 us
    pallas_call x1, Pallas kernels: 22 us -> 23.1 us  [local_channels(): pl.pallas_call(functools.partial(channel_kernel, count), out_shape=[block...]
where the time goes in v2:
time: 41.9 us; the launch traced here: 41.4 us
  Pallas kernels  23.1 us (55%)
  local copies, waits for them, and re-layouts  17.6 us (42%)
  between operations  0.67 us (2%)
    pallas_call x1, Pallas kernels, local_channels(): pl.pallas_call(functools.partial(channel_kernel, count), out_shape=[block...  23.1 us
    unnamed x36, local copies, waits for them, and re-layouts  17 us

profile of v2, /device:TPU:0, one launch (start us, length us, event | category | flops | bytes accessed | tf_op | source)
XLA Modules:
  0.0 41.4 jit_solution(6948137422337822814)
XLA Ops:
  0.6 0.0 copy-start
  0.6 0.9 %copy-done = bf16[256,512]{1,0:T(8,128)(2,1)S(1)} copy-done((bf16[256,512]{1,0:T(8,128)(2,1)S(1)}, bf16[256,512]{1,0:T(8,128)(2,1)}, u32[]{:S(2)}) %copy-start) | copy-done | bytes 262168
  1.6 0.0 copy-start.1
  1.6 0.9 %copy-done.1 = bf16[256,512]{1,0:T(8,128)(2,1)S(1)} copy-done((bf16[256,512]{1,0:T(8,128)(2,1)S(1)}, bf16[256,512]{1,0:T(8,128)(2,1)}, u32[]{:S(2)}) %copy-start.1) | copy-done | bytes 262168
  2.5 0.0 copy-start.2
  2.5 0.9 %copy-done.2 = bf16[512,256]{1,0:T(8,128)(2,1)S(1)} copy-done((bf16[512,256]{1,0:T(8,128)(2,1)S(1)}, bf16[512,256]{1,0:T(8,128)(2,1)}, u32[]{:S(2)}) %copy-start.2) | copy-done | bytes 262168
  3.5 0.0 copy-start.3
  3.5 0.9 %copy-done.3 = bf16[512,256]{1,0:T(8,128)(2,1)S(1)} copy-done((bf16[512,256]{1,0:T(8,128)(2,1)S(1)}, bf16[512,256]{1,0:T(8,128)(2,1)}, u32[]{:S(2)}) %copy-start.3) | copy-done | bytes 262168
  4.4 0.0 copy-start.4
  4.4 0.9 %copy-done.4 = bf16[16,4096]{1,0:T(8,128)(2,1)S(1)} copy-done((bf16[16,4096]{1,0:T(8,128)(2,1)S(1)}, bf16[16,4096]{1,0:T(8,128)(2,1)}, u32[]{:S(2)}) %copy-start.4) | copy-done | bytes 131096
  5.3 0.0 copy-start.5
  5.3 0.9 %copy-done.5 = bf16[16,4096]{1,0:T(8,128)(2,1)S(1)} copy-done((bf16[16,4096]{1,0:T(8,128)(2,1)S(1)}, bf16[16,4096]{1,0:T(8,128)(2,1)}, u32[]{:S(2)}) %copy-start.5) | copy-done | bytes 131096
  6.2 0.0 copy-start.6
  6.2 0.9 %copy-done.6 = bf16[16,4096]{1,0:T(8,128)(2,1)S(1)} copy-done((bf16[16,4096]{1,0:T(8,128)(2,1)S(1)}, bf16[16,4096]{1,0:T(8,128)(2,1)}, u32[]{:S(2)}) %copy-start.6) | copy-done | bytes 131096
  7.2 0.0 copy-start.7
  7.2 0.9 %copy-done.7 = bf16[16,4096]{1,0:T(8,128)(2,1)S(1)} copy-done((bf16[16,4096]{1,0:T(8,128)(2,1)S(1)}, bf16[16,4096]{1,0:T(8,128)(2,1)}, u32[]{:S(2)}) %copy-start.7) | copy-done | bytes 131096
  8.1 0.0 copy-start.8
  8.1 0.9 %copy-done.8 = bf16[16,4096]{1,0:T(8,128)(2,1)S(1)} copy-done((bf16[16,4096]{1,0:T(8,128)(2,1)S(1)}, bf16[16,4096]{1,0:T(8,128)(2,1)}, u32[]{:S(2)}) %copy-start.8) | copy-done | bytes 131096
  9.0 0.0 copy-start.9
  9.0 0.9 %copy-done.9 = f32[256,128]{1,0:T(8,128)S(1)} copy-done((f32[256,128]{1,0:T(8,128)S(1)}, f32[256,128]{1,0:T(8,128)}, u32[]{:S(2)}) %copy-start.9) | copy-done | bytes 131096
  9.9 0.0 copy-start.10
  9.9 0.9 %copy-done.10 = f32[256,128]{1,0:T(8,128)S(1)} copy-done((f32[256,128]{1,0:T(8,128)S(1)}, f32[256,128]{1,0:T(8,128)}, u32[]{:S(2)}) %copy-start.10) | copy-done | bytes 131096
  10.8 0.0 copy-start.11
  10.8 0.9 %copy-done.11 = bf16[256,256]{1,0:T(8,128)(2,1)S(1)} copy-done((bf16[256,256]{1,0:T(8,128)(2,1)S(1)}, bf16[256,256]{1,0:T(8,128)(2,1)}, u32[]{:S(2)}) %copy-start.11) | copy-done | bytes 131096
  11.7 0.0 copy-start.12
  11.7 0.9 %copy-done.12 = bf16[256,256]{1,0:T(8,128)(2,1)S(1)} copy-done((bf16[256,256]{1,0:T(8,128)(2,1)S(1)}, bf16[256,256]{1,0:T(8,128)(2,1)}, u32[]{:S(2)}) %copy-start.12) | copy-done | bytes 131096
  12.6 0.0 copy-start.13
  12.6 0.9 %copy-done.13 = bf16[256,256]{1,0:T(8,128)(2,1)S(1)} copy-done((bf16[256,256]{1,0:T(8,128)(2,1)S(1)}, bf16[256,256]{1,0:T(8,128)(2,1)}, u32[]{:S(2)}) %copy-start.13) | copy-done | bytes 131096
  13.5 0.0 copy-start.14
  13.5 0.9 %copy-done.14 = bf16[256,256]{1,0:T(8,128)(2,1)S(1)} copy-done((bf16[256,256]{1,0:T(8,128)(2,1)S(1)}, bf16[256,256]{1,0:T(8,128)(2,1)}, u32[]{:S(2)}) %copy-start.14) | copy-done | bytes 131096
  14.4 0.0 copy-start.15
  14.4 0.7 %copy-done.15 = f32[16]{0:T(128)S(1)} copy-done((f32[16]{0:T(128)S(1)}, f32[16]{0:T(128)}, u32[]{:S(2)}) %copy-start.15) | copy-done | bytes 88
  15.0 23.1 %shard_map.191 = (bf16[16,4096]{1,0:T(8,128)(2,1)S(1)}, bf16[16,4096]{1,0:T(8,128)(2,1)S(1)}, bf16[16,4096]{1,0:T(8,128)(2,1)S(1)}, bf16[16,4096]{1,0:T(8,128)(2,1)S(1)}, f32[16,128]{1,0:T(8,128)S(1)}) custom-call(bf16[16,4096]{1,0:T(8,128)(2,1)S(1)} %copy-done.4, bf16[16,4096]{1,0:T(8,128)(2,1)S(1)} %copy-done.5, bf16[16,4096]{1,0:T(8,128)(2,1)S(1)} %copy-done.6, ...), custom_call_target="tpu_custom_call" | custom-call | tf_op jit(solution)/shard_map/pallas_call | solution.py:443
  38.2 0.6 %slice_reduce_fusion = f32[16]{0:T(128)} fusion(f32[16,128]{1,0:T(8,128)S(1)} %get-tuple-element.14), kind=kLoop, calls=%fused_computation | loop fusion | bytes 128 | tf_op jit(solution)/shard_map/slice | solution.py:469
  38.8 0.7 %copy.25 = bf16[16,4096]{1,0:T(8,128)(2,1)} copy(bf16[16,4096]{1,0:T(8,128)(2,1)S(1)} %get-tuple-element.20) | data formatting | bytes 262144
  39.5 0.7 %copy.26 = bf16[16,4096]{1,0:T(8,128)(2,1)} copy(bf16[16,4096]{1,0:T(8,128)(2,1)S(1)} %get-tuple-element.21) | data formatting | bytes 262144
  40.1 0.7 %copy.27 = bf16[16,4096]{1,0:T(8,128)(2,1)} copy(bf16[16,4096]{1,0:T(8,128)(2,1)S(1)} %get-tuple-element.22) | data formatting | bytes 262144
  40.8 0.7 %copy.28 = bf16[16,4096]{1,0:T(8,128)(2,1)} copy(bf16[16,4096]{1,0:T(8,128)(2,1)S(1)} %get-tuple-element.23) | data formatting | bytes 262144
Async XLA Ops:
  0.6 1.0 %copy-start = (bf16[256,512]{1,0:T(8,128)(2,1)S(1)}, bf16[256,512]{1,0:T(8,128)(2,1)}, u32[]{:S(2)}) copy-start(bf16[256,512]{1,0:T(8,128)(2,1)} %constant.27.clone.refs_13_) | copy-start | bytes 786436
  1.6 0.9 %copy-start.1 = (bf16[256,512]{1,0:T(8,128)(2,1)S(1)}, bf16[256,512]{1,0:T(8,128)(2,1)}, u32[]{:S(2)}) copy-start(bf16[256,512]{1,0:T(8,128)(2,1)} %constant.26.clone.refs_12_) | copy-start | bytes 786436
  2.5 0.9 %copy-start.2 = (bf16[512,256]{1,0:T(8,128)(2,1)S(1)}, bf16[512,256]{1,0:T(8,128)(2,1)}, u32[]{:S(2)}) copy-start(bf16[512,256]{1,0:T(8,128)(2,1)} %constant.21.clone.refs_7_) | copy-start | bytes 786436
  3.5 0.9 %copy-start.3 = (bf16[512,256]{1,0:T(8,128)(2,1)S(1)}, bf16[512,256]{1,0:T(8,128)(2,1)}, u32[]{:S(2)}) copy-start(bf16[512,256]{1,0:T(8,128)(2,1)} %constant.20.clone.refs_6_) | copy-start | bytes 786436
  4.4 0.9 %copy-start.4 = (bf16[16,4096]{1,0:T(8,128)(2,1)S(1)}, bf16[16,4096]{1,0:T(8,128)(2,1)}, u32[]{:S(2)}) copy-start(bf16[16,4096]{1,0:T(8,128)(2,1)} %refs_0_.1) | copy-start | bytes 393220
  5.3 0.9 %copy-start.5 = (bf16[16,4096]{1,0:T(8,128)(2,1)S(1)}, bf16[16,4096]{1,0:T(8,128)(2,1)}, u32[]{:S(2)}) copy-start(bf16[16,4096]{1,0:T(8,128)(2,1)} %refs_1_.1) | copy-start | bytes 393220
  6.2 0.9 %copy-start.6 = (bf16[16,4096]{1,0:T(8,128)(2,1)S(1)}, bf16[16,4096]{1,0:T(8,128)(2,1)}, u32[]{:S(2)}) copy-start(bf16[16,4096]{1,0:T(8,128)(2,1)} %refs_2_.1) | copy-start | bytes 393220
  7.2 0.9 %copy-start.7 = (bf16[16,4096]{1,0:T(8,128)(2,1)S(1)}, bf16[16,4096]{1,0:T(8,128)(2,1)}, u32[]{:S(2)}) copy-start(bf16[16,4096]{1,0:T(8,128)(2,1)} %refs_3_.1) | copy-start | bytes 393220
  8.1 0.9 %copy-start.8 = (bf16[16,4096]{1,0:T(8,128)(2,1)S(1)}, bf16[16,4096]{1,0:T(8,128)(2,1)}, u32[]{:S(2)}) copy-start(bf16[16,4096]{1,0:T(8,128)(2,1)} %refs_4_.1) | copy-start | bytes 393220
  9.0 0.9 %copy-start.9 = (f32[256,128]{1,0:T(8,128)S(1)}, f32[256,128]{1,0:T(8,128)}, u32[]{:S(2)}) copy-start(f32[256,128]{1,0:T(8,128)} %constant.29.clone.refs_15_) | copy-start | bytes 393220
  9.9 0.9 %copy-start.10 = (f32[256,128]{1,0:T(8,128)S(1)}, f32[256,128]{1,0:T(8,128)}, u32[]{:S(2)}) copy-start(f32[256,128]{1,0:T(8,128)} %constant.28.clone.refs_14_) | copy-start | bytes 393220
  10.8 0.9 %copy-start.11 = (bf16[256,256]{1,0:T(8,128)(2,1)S(1)}, bf16[256,256]{1,0:T(8,128)(2,1)}, u32[]{:S(2)}) copy-start(bf16[256,256]{1,0:T(8,128)(2,1)} %constant.25.clone.refs_11_) | copy-start | bytes 393220
  11.7 0.9 %copy-start.12 = (bf16[256,256]{1,0:T(8,128)(2,1)S(1)}, bf16[256,256]{1,0:T(8,128)(2,1)}, u32[]{:S(2)}) copy-start(bf16[256,256]{1,0:T(8,128)(2,1)} %constant.24.clone.refs_10_) | copy-start | bytes 393220
  12.6 0.9 %copy-start.13 = (bf16[256,256]{1,0:T(8,128)(2,1)S(1)}, bf16[256,256]{1,0:T(8,128)(2,1)}, u32[]{:S(2)}) copy-start(bf16[256,256]{1,0:T(8,128)(2,1)} %constant.23.clone.refs_9_) | copy-start | bytes 393220
  13.5 0.9 %copy-start.14 = (bf16[256,256]{1,0:T(8,128)(2,1)S(1)}, bf16[256,256]{1,0:T(8,128)(2,1)}, u32[]{:S(2)}) copy-start(bf16[256,256]{1,0:T(8,128)(2,1)} %constant.22.clone.refs_8_) | copy-start | bytes 393220
  14.4 0.7 %copy-start.15 = (f32[16]{0:T(128)S(1)}, f32[16]{0:T(128)}, u32[]{:S(2)}) copy-start(f32[16]{0:T(128)} %refs_5_.1) | copy-start | bytes 196

commit v3 on v2

--- a/solution.py
+++ b/solution.py
@@ -227,7 +227,7 @@
 def halves(table):
     high = table.astype(np.float32).astype(ml_dtypes.bfloat16)
     low = (table - high.astype(np.float64)).astype(np.float32).astype(ml_dtypes.bfloat16)
-    return jnp.asarray(high), jnp.asarray(low)
+    return high, low
 
 
 def transform_tables(rows):
@@ -240,14 +240,11 @@
     second = np.block([[np.cos(inner), -np.sin(inner)], [np.sin(inner), np.cos(inner)]])
     second_back = np.block([[np.cos(inner), np.sin(inner)], [-np.sin(inner), np.cos(inner)]])
     first_back = np.concatenate([np.cos(outer.T), -np.sin(outer.T)], axis=1) / total
-    return (
-        *halves(first),
-        *halves(second),
-        *halves(second_back),
-        *halves(first_back),
-        jnp.asarray(np.cos(turn).astype(np.float32)),
-        jnp.asarray(np.sin(turn).astype(np.float32)),
-    )
+    parts = halves(first) + halves(second) + halves(second_back)
+    for table in halves(first_back):
+        parts += (table[:, :rows], table[:, rows:])
+    turns = np.concatenate([np.cos(turn), np.sin(turn)]).astype(np.float32)
+    return jnp.asarray(np.concatenate(parts)), jnp.asarray(turns)
 
 
 def split(value):
@@ -264,12 +261,12 @@
     count,
     *refs,
 ):
-    args, gain_ref, tables, refs = refs[:5], refs[5], refs[6:16], refs[16:]
+    args, gain_ref, tables, refs = refs[:5], refs[5], refs[6:8], refs[8:]
     gq_ref, gk_ref, gv_ref, gf_ref, skip_ref = refs[:5]
-    arg_vmem, table_vmem, refs = refs[5:10], refs[10:20], refs[20:]
+    arg_vmem, table_vmem, refs = refs[5:10], refs[10:12], refs[12:]
     out_box, in_box, res_box, got_box, sum_box, sum_got = refs[:6]
     send_in, recv_in, send_res, recv_res, send_sum, recv_sum, load_sem = refs[6:]
-    first_h, first_l, second_h, second_l, back2_h, back2_l, back1_h, back1_l, cos_ref, sin_ref = table_vmem
+    table_ref, turn_ref = table_vmem
     me = lax.axis_index("seq")
     chans, tok_local = args[0].shape
     per = chans // count
@@ -343,6 +340,9 @@
     for load in loads[5:]:
         load.wait()
 
+    def table(first, blocks=1):
+        return table_ref[first * rows : (first + blocks) * rows]
+
     def one_channel(chan, carry):
         for step in range(1, count):
             send_copy(chan, step).wait_recv()
@@ -356,16 +356,16 @@
 
         high = jnp.concatenate([mixed_h, gated_h], axis=1)
         low = jnp.concatenate([mixed_l, gated_l], axis=1)
-        pair = dot(first_h[...], high) + dot(first_h[...], low) + dot(first_l[...], high)
-        both = dot(jnp.concatenate([first_h[...], first_l[...]], axis=0), taps)
+        pair = dot(table(0, 2), high) + dot(table(0, 2), low) + dot(table(2, 2), high)
+        both = dot(table(0, 4), taps)
         tap_out = both[: 2 * rows] + both[2 * rows :]
-        cosine, sine = cos_ref[...], sin_ref[...]
+        cosine, sine = turn_ref[:rows], turn_ref[rows:]
         turned = []
         for block in (pair[:, :LANES], pair[:, LANES:], tap_out):
             real, imag = block[:rows], block[rows:]
             turned.append(jnp.concatenate([real * cosine + imag * sine, imag * cosine - real * sine], axis=1))
         work_h, work_l = split(jnp.concatenate(turned, axis=0))
-        spec = dot(work_h, second_h[...]) + dot(work_l, second_h[...]) + dot(work_h, second_l[...])
+        spec = dot(work_h, table(4)) + dot(work_l, table(4)) + dot(work_h, table(5))
         mix_re, mix_im = spec[:rows, :LANES], spec[:rows, LANES:]
         grad_re, grad_im = spec[rows : 2 * rows, :LANES], spec[rows : 2 * rows, LANES:]
         ker_re, ker_im = spec[2 * rows :, :LANES], spec[2 * rows :, LANES:]
@@ -378,14 +378,17 @@
             axis=0,
         )
         prod_h, prod_l = split(prods)
-        work = dot(prod_h, back2_h[...]) + dot(prod_l, back2_h[...]) + dot(prod_h, back2_l[...])
-        turned = []
+        work = dot(prod_h, table(6)) + dot(prod_l, table(6)) + dot(prod_h, table(7))
+        turned_re, turned_im = [], []
         for block in range(3):
             real = work[block * rows : (block + 1) * rows, :LANES]
             imag = work[block * rows : (block + 1) * rows, LANES:]
-            turned.append(jnp.concatenate([real * cosine - imag * sine, imag * cosine + real * sine], axis=0))
-        work_h, work_l = split(jnp.concatenate(turned, axis=1))
-        result = dot(back1_h[...], work_h) + dot(back1_h[...], work_l) + dot(back1_l[...], work_h)
+            turned_re.append(real * cosine - imag * sine)
+            turned_im.append(imag * cosine + real * sine)
+        real_h, real_l = split(jnp.concatenate(turned_re, axis=1))
+        imag_h, imag_l = split(jnp.concatenate(turned_im, axis=1))
+        result = dot(table(8), real_h) + dot(table(8), real_l) + dot(table(10), real_h)
+        result = result + dot(table(9), imag_h) + dot(table(9), imag_l) + dot(table(11), imag_h)
         convolved, carried, lag_grad = [result[:, i * LANES : (i + 1) * LANES] for i in range(3)]
 
         gain = gain_ref[me * per + chan]
@@ -443,7 +446,7 @@
     *grads, skips = pl.pallas_call(
         functools.partial(channel_kernel, count),
         out_shape=[block] * 4 + [jax.ShapeDtypeStruct((chans, LANES), jnp.float32)],
-        in_specs=[hbm] * 5 + [smem] + [hbm] * 10,
+        in_specs=[hbm] * 5 + [smem] + [hbm] * 2,
         out_specs=[vmem] * 5,
         scratch_shapes=[
             *[pltpu.VMEM((chans, tok_local), jnp.bfloat16) for _ in range(5)],
@@ -460,10 +463,10 @@
             dma((per, count)),
             dma((count,)),
             dma((count,)),
-            dma((15,)),
+            dma((7,)),
         ],
         compiler_params=pltpu.CompilerParams(
-            collective_id=0, has_side_effects=True, vmem_limit_bytes=48 * 1024 * 1024
+            collective_id=0, has_side_effects=True, vmem_limit_bytes=63 * 1024 * 1024
         ),
     )(queries, key_proj, value_proj, cotangent, filter_taps, skip_gain, *tables)
     return (*grads, skips[:, 0])
@@ -473,7 +476,7 @@
     count = lax.axis_size("seq")
     chans, tok_local = arguments[0].shape
     whole_channels = chans % count == 0 and count & (count - 1) == 0
-    if whole_channels and count > 1 and tok_local % (16 * LANES) == 0 and count * tok_local <= 65536:
+    if whole_channels and count > 1 and tok_local % (16 * LANES) == 0 and count * tok_local == 2 * LANES * LANES:
         return local_channels(*arguments)
     return local_butterfly(*arguments)
 

time: 41.9 us -> 31.3 us (0.75)
  local copies, waits for them, and re-layouts: 17.6 us -> 7.59 us
    unnamed x36 -> x4, local copies, waits for them, and re-layouts: 17 us -> 6.27 us
    slice x1, local copies, waits for them, and re-layouts: 0.63 us -> 1.32 us  [local_channels(): return (*grads, skips[:, 0])]
where the time goes in v3:
time: 31.3 us; the launch traced here: 31.1 us
  Pallas kernels  22.9 us (73%)
  local copies, waits for them, and re-layouts  7.59 us (24%)
  between operations  0.64 us (2%)
    pallas_call x1, Pallas kernels, local_channels(): pl.pallas_call(functools.partial(channel_kernel, count), out_shape=[block...  22.9 us
    unnamed x4, local copies, waits for them, and re-layouts  6.27 us
    slice x1, local copies, waits for them, and re-layouts, local_channels(): return (*grads, skips[:, 0])  1.32 us

profile of v3, /device:TPU:0, one launch (start us, length us, event | category | flops | bytes accessed | tf_op | source)
XLA Modules:
  0.0 31.1 jit_solution(4999632283990719523)
XLA Ops:
  0.6 22.9 %shard_map.119 = (bf16[16,4096]{1,0:T(8,128)(2,1)}, bf16[16,4096]{1,0:T(8,128)(2,1)}, bf16[16,4096]{1,0:T(8,128)(2,1)}, bf16[16,4096]{1,0:T(8,128)(2,1)}, f32[16,128]{1,0:T(8,128)}) custom-call(bf16[16,4096]{1,0:T(8,128)(2,1)} %refs_0_.1, bf16[16,4096]{1,0:T(8,128)(2,1)} %refs_1_.1, bf16[16,4096]{1,0:T(8,128)(2,1)} %refs_2_.1, bf16[16,4096]{1,0:T(8,128)(2,1)} %refs_3_.1, ...), custom_call_target="tpu_custom_call" | custom-call | tf_op jit(solution)/shard_map/pallas_call | solution.py:446
  23.5 1.3 %slice_reduce_fusion = f32[16]{0:T(128)} fusion(f32[16,128]{1,0:T(8,128)} %get-tuple-element.14), kind=kLoop, calls=%fused_computation | loop fusion | bytes 128 | tf_op jit(solution)/shard_map/slice | solution.py:472
  24.8 1.6 %copy.17 = bf16[16,4096]{1,0:T(8,128)(2,1)} copy(bf16[16,4096]{1,0:T(8,128)(2,1)} %get-tuple-element.20) | data formatting | bytes 262144
  26.4 1.6 %copy.18 = bf16[16,4096]{1,0:T(8,128)(2,1)} copy(bf16[16,4096]{1,0:T(8,128)(2,1)} %get-tuple-element.21) | data formatting | bytes 262144
  27.9 1.6 %copy.19 = bf16[16,4096]{1,0:T(8,128)(2,1)} copy(bf16[16,4096]{1,0:T(8,128)(2,1)} %get-tuple-element.22) | data formatting | bytes 262144
  29.5 1.6 %copy.20 = bf16[16,4096]{1,0:T(8,128)(2,1)} copy(bf16[16,4096]{1,0:T(8,128)(2,1)} %get-tuple-element.23) | data formatting | bytes 262144

commit v4 on v3

--- a/solution.py
+++ b/solution.py
@@ -262,10 +262,10 @@
     *refs,
 ):
     args, gain_ref, tables, refs = refs[:5], refs[5], refs[6:8], refs[8:]
-    gq_ref, gk_ref, gv_ref, gf_ref, skip_ref = refs[:5]
-    arg_vmem, table_vmem, refs = refs[5:10], refs[10:12], refs[12:]
-    out_box, in_box, res_box, got_box, sum_box, sum_got = refs[:6]
-    send_in, recv_in, send_res, recv_res, send_sum, recv_sum, load_sem = refs[6:]
+    got_box, sum_got = refs[:2]
+    arg_vmem, table_vmem, refs = refs[2:7], refs[7:9], refs[9:]
+    out_box, in_box, res_box, sum_box = refs[:4]
+    send_in, recv_in, send_res, recv_res, send_sum, recv_sum, load_sem, own_sem = refs[4:]
     table_ref, turn_ref = table_vmem
     me = lax.axis_index("seq")
     chans, tok_local = args[0].shape
@@ -274,6 +274,10 @@
     rows = part * count
     norm_scale = 1.0 / math.sqrt(rows * LANES)
 
+    barrier = pltpu.get_barrier_semaphore()
+    for step in range(1, count):
+        pl.semaphore_signal(barrier, inc=1, device_id={"seq": me ^ step}, device_id_type=pl.DeviceIdType.MESH)
+
     loads = [
         pltpu.make_async_copy(source, target, load_sem.at[i])
         for i, (source, target) in enumerate(zip(args + tables, arg_vmem + table_vmem))
@@ -283,10 +287,6 @@
 
     def peer_of(step):
         return me ^ step
-
-    barrier = pltpu.get_barrier_semaphore()
-    for step in range(1, count):
-        pl.semaphore_signal(barrier, inc=1, device_id={"seq": peer_of(step)}, device_id_type=pl.DeviceIdType.MESH)
 
     for load in loads[5:]:
         load.start()
@@ -320,6 +320,9 @@
             device_id_type=pl.DeviceIdType.MESH,
         )
 
+    def own_result(chan):
+        return pltpu.make_async_copy(res_box.at[chan, me], got_box.at[me, chan], own_sem.at[chan])
+
     def sum_copy(step):
         peer = peer_of(step)
         return pltpu.make_async_remote_copy(
@@ -336,6 +339,17 @@
             send_copy(chan, step).start()
     for chan in range(per):
         in_box[chan, me] = out_box[me, chan]
+
+    query_f, key_f, value_f, cot_f = [ref[...].astype(jnp.float32) for ref in arg_vmem[:4]]
+    column = jnp.sum((cot_f * query_f) * (key_f * value_f), axis=1, keepdims=True) * norm_scale
+    lane = lax.broadcasted_iota(jnp.int32, (chans, LANES), 1)
+    row = lax.broadcasted_iota(jnp.int32, (chans, LANES), 0)
+    spread = jnp.sum(jnp.where(lane == row, column, 0.0), axis=0, keepdims=True)
+    sum_box[...] = jnp.broadcast_to(spread, (8, LANES))
+    for step in range(1, count):
+        sum_copy(step).start()
+    own_sum = pltpu.make_async_copy(sum_box, sum_got.at[me], own_sem.at[per])
+    own_sum.start()
 
     for load in loads[5:]:
         load.wait()
@@ -403,32 +417,44 @@
             res_box[chan, :, slot] = value.astype(jnp.bfloat16).reshape(count, part, LANES)
         for step in reversed(range(1, count)):
             result_copy(chan, step).start()
-        total = jnp.sum(jnp.sum(gated * mixed, axis=0, keepdims=True), axis=1, keepdims=True) * norm_scale
-        sum_box[chan] = jnp.broadcast_to(total, (8, LANES))
+        own_result(chan).start()
         return carry
 
     lax.fori_loop(0, per, one_channel, 0)
 
-    for step in range(1, count):
-        sum_copy(step).start()
-    for chan in range(per):
-        got_box[me, chan] = res_box[chan, me]
-    sum_got[me] = sum_box[...]
     for chan in range(per):
         for step in range(1, count):
             send_copy(chan, step).wait_send()
+    own_sum.wait()
     for step in range(1, count):
         sum_copy(step).wait()
     for chan in range(per):
+        own_result(chan).wait()
         for step in range(1, count):
             result_copy(chan, step).wait()
 
-    for slot, ref in enumerate((gq_ref, gk_ref, gv_ref, gf_ref)):
-        pieces = got_box[:, :, slot].reshape(chans, part, LANES).astype(jnp.float32)
+
+def finish_kernel(got_ref, sum_ref, *refs):
+    outs, skip_ref = refs[:4], refs[4]
+    got_vmem, out_vmem, load_sem, store_sem = refs[5:]
+    count, per, _, part, _ = got_ref.shape
+    chans = count * per
+    loads = [
+        pltpu.make_async_copy(got_ref.at[:, :, slot], got_vmem.at[slot], load_sem.at[slot]) for slot in range(4)
+    ]
+    stores = [pltpu.make_async_copy(out_vmem.at[slot], outs[slot], store_sem.at[slot]) for slot in range(4)]
+    for load in loads:
+        load.start()
+    skip_ref[...] = jnp.sum(sum_ref[...], axis=0)[0, :chans]
+    for slot in range(4):
+        loads[slot].wait()
+        pieces = got_vmem[slot].reshape(chans, part, LANES).astype(jnp.float32)
         turned = jnp.swapaxes(pieces, 0, 1).astype(jnp.bfloat16)
         for r in range(part):
-            ref[:, r * LANES : (r + 1) * LANES] = turned[r]
-    skip_ref[...] = sum_got[...].reshape(chans, 8, LANES)[:, 0, :]
+            out_vmem[slot, :, r * LANES : (r + 1) * LANES] = turned[r]
+        stores[slot].start()
+    for store in stores:
+        store.wait()
 
 
 def local_channels(queries, key_proj, value_proj, cotangent, filter_taps, skip_gain):
@@ -443,20 +469,21 @@
     smem = pl.BlockSpec(memory_space=pltpu.SMEM)
     block = jax.ShapeDtypeStruct((chans, tok_local), jnp.bfloat16)
     dma = pltpu.SemaphoreType.DMA
-    *grads, skips = pl.pallas_call(
+    got, sums = pl.pallas_call(
         functools.partial(channel_kernel, count),
-        out_shape=[block] * 4 + [jax.ShapeDtypeStruct((chans, LANES), jnp.float32)],
+        out_shape=[
+            jax.ShapeDtypeStruct((count, per, 4, part, LANES), jnp.bfloat16),
+            jax.ShapeDtypeStruct((count, 8, LANES), jnp.float32),
+        ],
         in_specs=[hbm] * 5 + [smem] + [hbm] * 2,
-        out_specs=[vmem] * 5,
+        out_specs=[hbm] * 2,
         scratch_shapes=[
             *[pltpu.VMEM((chans, tok_local), jnp.bfloat16) for _ in range(5)],
             *[pltpu.VMEM(table.shape, table.dtype) for table in tables],
             pltpu.VMEM((count, per, 5, part, LANES), jnp.bfloat16),
             pltpu.VMEM((per, count, 5, part, LANES), jnp.bfloat16),
             pltpu.VMEM((per, count, 4, part, LANES), jnp.bfloat16),
-            pltpu.VMEM((count, per, 4, part, LANES), jnp.bfloat16),
-            pltpu.VMEM((per, 8, LANES), jnp.float32),
-            pltpu.VMEM((count, per, 8, LANES), jnp.float32),
+            pltpu.VMEM((8, LANES), jnp.float32),
             dma((per, count)),
             dma((per, count)),
             dma((per, count)),
@@ -464,12 +491,25 @@
             dma((count,)),
             dma((count,)),
             dma((7,)),
+            dma((per + 1,)),
         ],
         compiler_params=pltpu.CompilerParams(
             collective_id=0, has_side_effects=True, vmem_limit_bytes=63 * 1024 * 1024
         ),
     )(queries, key_proj, value_proj, cotangent, filter_taps, skip_gain, *tables)
-    return (*grads, skips[:, 0])
+    return pl.pallas_call(
+        finish_kernel,
+        out_shape=[block] * 4 + [jax.ShapeDtypeStruct((chans,), jnp.float32)],
+        in_specs=[hbm, vmem],
+        out_specs=[hbm] * 4 + [vmem],
+        scratch_shapes=[
+            pltpu.VMEM((4, count, per, part, LANES), jnp.bfloat16),
+            pltpu.VMEM((4, chans, tok_local), jnp.bfloat16),
+            dma((4,)),
+            dma((4,)),
+        ],
+        compiler_params=pltpu.CompilerParams(vmem_limit_bytes=63 * 1024 * 1024),
+    )(got, sums)
 
 
 def local(*arguments):

time: 31.3 us -> 25.6 us (0.82)
  local copies, waits for them, and re-layouts: 7.59 us -> 0 us
  Pallas kernels: 22.9 us -> 24.8 us
    unnamed x4 -> x0, local copies, waits for them, and re-layouts: 6.27 us -> none
    pallas_call x1 -> x2, Pallas kernels: 22.9 us -> 24.8 us  [the longest x1 21.6 us: local_channels(): pl.pallas_call(functools.partial(channel_kernel, count), out_shape=[jax.S...]
    slice x1 -> x0, local copies, waits for them, and re-layouts: 1.32 us -> none  [local_channels(): return (*grads, skips[:, 0])]
where the time goes in v4:
time: 25.6 us; the launch traced here: 25.4 us
  Pallas kernels  24.8 us (97%)
  between operations  0.64 us (2%)
    pallas_call x1, Pallas kernels, local_channels(): pl.pallas_call(functools.partial(channel_kernel, count), out_shape=[jax.S...  21.6 us
    pallas_call x1, Pallas kernels, local_channels(): pl.pallas_call(finish_kernel, out_shape=[block] * 4 + [jax.ShapeDtypeStru...  3.15 us

profile of v4, /device:TPU:0, one launch (start us, length us, event | category | flops | bytes accessed | tf_op | source)
XLA Modules:
  0.0 25.4 jit_solution(1596433540105856095)
XLA Ops:
  0.6 21.6 %shard_map.119 = (bf16[8,2,4,32,128]{4,3,2,1,0:T(8,128)(2,1)}, f32[8,8,128]{2,1,0:T(8,128)}) custom-call(bf16[16,4096]{1,0:T(8,128)(2,1)} %refs_0_.1, bf16[16,4096]{1,0:T(8,128)(2,1)} %refs_1_.1, bf16[16,4096]{1,0:T(8,128)(2,1)} %refs_2_.1, bf16[16,4096]{1,0:T(8,128)(2,1)} %refs_3_.1, bf16[16,4096]{1,0:T(8,128)(2,1)} %refs_4_.1, f32[16]{0:T(128)} %refs_5_.1, ...), custom_call_target="tpu_custom_call" | custom-call | tf_op jit(solution)/shard_map/pallas_call | solution.py:472
  22.2 3.1 %shard_map.120 = (bf16[16,4096]{1,0:T(8,128)(2,1)}, bf16[16,4096]{1,0:T(8,128)(2,1)}, bf16[16,4096]{1,0:T(8,128)(2,1)}, bf16[16,4096]{1,0:T(8,128)(2,1)}, f32[16]{0:T(128)}) custom-call(bf16[8,2,4,32,128]{4,3,2,1,0:T(8,128)(2,1)} %get-tuple-element.7.got_ref, f32[8,8,128]{2,1,0:T(8,128)} %get-tuple-element.8.sum_ref), custom_call_target="tpu_custom_call" | custom-call | tf_op jit(solution)/shard_map/pallas_call | solution.py:500

commit v5 on v4

--- a/solution.py
+++ b/solution.py
@@ -436,19 +436,13 @@
 
 def finish_kernel(got_ref, sum_ref, *refs):
     outs, skip_ref = refs[:4], refs[4]
-    got_vmem, out_vmem, load_sem, store_sem = refs[5:]
+    out_vmem, store_sem = refs[5:]
     count, per, _, part, _ = got_ref.shape
     chans = count * per
-    loads = [
-        pltpu.make_async_copy(got_ref.at[:, :, slot], got_vmem.at[slot], load_sem.at[slot]) for slot in range(4)
-    ]
     stores = [pltpu.make_async_copy(out_vmem.at[slot], outs[slot], store_sem.at[slot]) for slot in range(4)]
-    for load in loads:
-        load.start()
     skip_ref[...] = jnp.sum(sum_ref[...], axis=0)[0, :chans]
     for slot in range(4):
-        loads[slot].wait()
-        pieces = got_vmem[slot].reshape(chans, part, LANES).astype(jnp.float32)
+        pieces = got_ref[:, :, slot].reshape(chans, part, LANES).astype(jnp.float32)
         turned = jnp.swapaxes(pieces, 0, 1).astype(jnp.bfloat16)
         for r in range(part):
             out_vmem[slot, :, r * LANES : (r + 1) * LANES] = turned[r]
@@ -472,11 +466,11 @@
     got, sums = pl.pallas_call(
         functools.partial(channel_kernel, count),
         out_shape=[
-            jax.ShapeDtypeStruct((count, per, 4, part, LANES), jnp.bfloat16),
-            jax.ShapeDtypeStruct((count, 8, LANES), jnp.float32),
+            pltpu.VMEM((count, per, 4, part, LANES), jnp.bfloat16),
+            pltpu.VMEM((count, 8, LANES), jnp.float32),
         ],
         in_specs=[hbm] * 5 + [smem] + [hbm] * 2,
-        out_specs=[hbm] * 2,
+        out_specs=[vmem] * 2,
         scratch_shapes=[
             *[pltpu.VMEM((chans, tok_local), jnp.bfloat16) for _ in range(5)],
             *[pltpu.VMEM(table.shape, table.dtype) for table in tables],
@@ -494,21 +488,19 @@
             dma((per + 1,)),
         ],
         compiler_params=pltpu.CompilerParams(
-            collective_id=0, has_side_effects=True, vmem_limit_bytes=63 * 1024 * 1024
+            collective_id=0, has_side_effects=True, vmem_limit_bytes=(64 * 1024 - 896) * 1024
         ),
     )(queries, key_proj, value_proj, cotangent, filter_taps, skip_gain, *tables)
     return pl.pallas_call(
         finish_kernel,
         out_shape=[block] * 4 + [jax.ShapeDtypeStruct((chans,), jnp.float32)],
-        in_specs=[hbm, vmem],
+        in_specs=[vmem, vmem],
         out_specs=[hbm] * 4 + [vmem],
         scratch_shapes=[
-            pltpu.VMEM((4, count, per, part, LANES), jnp.bfloat16),
             pltpu.VMEM((4, chans, tok_local), jnp.bfloat16),
             dma((4,)),
-            dma((4,)),
         ],
-        compiler_params=pltpu.CompilerParams(vmem_limit_bytes=63 * 1024 * 1024),
+        compiler_params=pltpu.CompilerParams(vmem_limit_bytes=32 * 1024 * 1024),
     )(got, sums)
 
 

time: 25.6 us -> 23.6 us (0.922)
  Pallas kernels: 24.8 us -> 22.8 us
    pallas_call x1, Pallas kernels: 3.15 us -> 1.43 us  [local_channels(): pl.pallas_call(finish_kernel, out_shape=[block] * 4 + [jax.ShapeDtypeStru...]
where the time goes in v5:
time: 23.6 us; the launch traced here: 23.5 us
  Pallas kernels  22.8 us (97%)
  between operations  0.64 us (3%)
    pallas_call x1, Pallas kernels, local_channels(): pl.pallas_call(functools.partial(channel_kernel, count), out_shape=[pltpu...  21.4 us
    pallas_call x1, Pallas kernels, local_channels(): pl.pallas_call(finish_kernel, out_shape=[block] * 4 + [jax.ShapeDtypeStru...  1.43 us

profile of v5, /device:TPU:0, one launch (start us, length us, event | category | flops | bytes accessed | tf_op | source)
XLA Modules:
  0.0 23.5 jit_solution(3400211337442177956)
XLA Ops:
  0.6 21.4 %shard_map.119 = (bf16[8,2,4,32,128]{4,3,2,1,0:T(8,128)(2,1)S(1)}, f32[8,8,128]{2,1,0:T(8,128)S(1)}) custom-call(bf16[16,4096]{1,0:T(8,128)(2,1)} %refs_0_.1, bf16[16,4096]{1,0:T(8,128)(2,1)} %refs_1_.1, bf16[16,4096]{1,0:T(8,128)(2,1)} %refs_2_.1, bf16[16,4096]{1,0:T(8,128)(2,1)} %refs_3_.1, bf16[16,4096]{1,0:T(8,128)(2,1)} %refs_4_.1, f32[16]{0:T(128)} %refs_5_.1, ...), custom_call_target="tpu_custom_call" | custom-call | tf_op jit(solution)/shard_map/pallas_call | solution.py:466
  22.0 1.4 %shard_map.120 = (bf16[16,4096]{1,0:T(8,128)(2,1)}, bf16[16,4096]{1,0:T(8,128)(2,1)}, bf16[16,4096]{1,0:T(8,128)(2,1)}, bf16[16,4096]{1,0:T(8,128)(2,1)}, f32[16]{0:T(128)}) custom-call(bf16[8,2,4,32,128]{4,3,2,1,0:T(8,128)(2,1)S(1)} %get-tuple-element.7.got_ref, f32[8,8,128]{2,1,0:T(8,128)S(1)} %get-tuple-element.8.sum_ref), custom_call_target="tpu_custom_call" | custom-call | tf_op jit(solution)/shard_map/pallas_call | solution.py:494
